TPU v7x, 32 devices: a whole 2x2x4 slice. The times are simulated.
32 devices in a mesh: img: 8 (over z, y), blk: 4 (over x, core).
Axes of the slice: x: 2, y: 2, z: 4, core: 2. Of those that a mesh axis runs over, the one named last changes fastest.
Arguments:
- tokens: bfloat16 [24, 1024, 768], P('img', 'blk'), may hold values from -6 to 6
- counts: int32 [24], P('img'), may hold values from 64 to 1024, as said below
- qkv_weight: bfloat16 [768, 2304], replicated, may hold values from -0.21875 to 0.21875
- q_bias: bfloat16 [768], replicated, may hold values from -3 to 3
- v_bias: bfloat16 [768], replicated, may hold values from -3 to 3
- out_weight: bfloat16 [768, 768], replicated, may hold values from -0.875 to 0.875
- out_bias: bfloat16 [768], replicated, may hold values from -2 to 2
- norm1_gain: bfloat16 [768], replicated, may hold values from 0.5 to 1.5
- norm1_bias: bfloat16 [768], replicated, may hold values from -2 to 2
- norm2_gain: bfloat16 [768], replicated, may hold values from 0.5 to 1.5
- norm2_bias: bfloat16 [768], replicated, may hold values from -2 to 2
- fc1_weight: bfloat16 [768, 3072], replicated, may hold values from -0.21875 to 0.21875
- fc1_bias: bfloat16 [3072], replicated, may hold values from -3 to 3
- fc2_weight: bfloat16 [3072, 768], replicated, may hold values from -0.109375 to 0.109375
- fc2_bias: bfloat16 [768], replicated, may hold values from -2 to 2
- scale1: bfloat16 [768], replicated, may hold values from 0.5 to 1.5
- scale2: bfloat16 [768], replicated, may hold values from 0.5 to 1.5
- cotangent: bfloat16 [24, 1024, 768], P('img', 'blk'), may hold values from -6 to 6
Outputs:
- output: bfloat16 [24, 1024, 768], P('img', 'blk')
- grad_tokens: bfloat16 [24, 1024, 768], P('img', 'blk')
- grad_qkv_weight: float32 [768, 2304], P(('img', 'blk'))
- grad_q_bias: float32 [768], P(('img', 'blk'))
- grad_v_bias: float32 [768], P(('img', 'blk'))
- grad_out_weight: float32 [768, 768], P(('img', 'blk'))
- grad_out_bias: float32 [768], P(('img', 'blk'))
- grad_norm1_gain: float32 [768], P(('img', 'blk'))
- grad_norm1_bias: float32 [768], P(('img', 'blk'))
- grad_norm2_gain: float32 [768], P(('img', 'blk'))
- grad_norm2_bias: float32 [768], P(('img', 'blk'))
- grad_fc1_weight: float32 [768, 3072], P(('img', 'blk'))
- grad_fc1_bias: float32 [3072], P(('img', 'blk'))
- grad_fc2_weight: float32 [3072, 768], P(('img', 'blk'))
- grad_fc2_bias: float32 [768], P(('img', 'blk'))
- grad_scale1: float32 [768], P(('img', 'blk'))
- grad_scale2: float32 [768], P(('img', 'blk'))
Inputs may be any that keep to these rules, and one draw needn't show every extreme that they name: The first counts[i] rows of image i are valid patches and the rest are padding; in each aligned group of 3 images one image has all 1024 rows valid.
All inputs are finite; a program needn't handle non-finite values.
Results may differ from a plain program's by a relative error of at most 0.015.
Values may be sent and summed in bfloat16 or wider, within the bound.
A program may use at most 192 MiB of HBM per device.

v0:
```python
from functools import partial

import jax
import jax.numpy as jnp
from jax import lax
from jax.sharding import PartitionSpec as P

HEADS = 12


score_scale = 0.125
norm_eps = 1e-06
masked_value = -1e30


def layer_norm(vector, norm_gain, norm_shift):
    average = jnp.mean(vector, axis=-1, keepdims=True)
    centered = vector - average
    spread = jnp.mean(centered * centered, axis=-1, keepdims=True)
    return centered * lax.rsqrt(spread + norm_eps) * norm_gain + norm_shift


def gelu_exact(vector):
    return jax.nn.gelu(vector, approximate=False)


def left_dot(left_side, right_side):
    return lax.dot_general(
        left_side, right_side, (((0,), (0,)), ((), ())), preferred_element_type=jnp.float32
    )


def right_dot(left_side, right_side):
    return lax.dot_general(
        left_side, right_side, (((1,), (1,)), ((), ())), preferred_element_type=jnp.float32
    )


def split_heads(matrix):
    return matrix.reshape(matrix.shape[:-1] + (HEADS, matrix.shape[-1] // HEADS))


def absorb(query_heads, counts, carry, piece, start):
    peak_score, weight_sum, weighted = carry
    key_heads = split_heads(piece[0])
    value_heads = split_heads(piece[1])
    raw_scores = jnp.einsum(
        "bqhd,bkhd->bhqk", query_heads, key_heads, preferred_element_type=jnp.float32
    )
    positions = jnp.arange(piece[0].shape[1], dtype=jnp.int32)
    valid_keys = positions[None, :] < counts[:, None]
    scores = jnp.where(valid_keys[:, None, None, :], raw_scores * score_scale, masked_value)
    new_peak = jnp.maximum(peak_score, jnp.max(scores, axis=-1))
    rescale = jnp.exp(peak_score - new_peak)
    weights = jnp.exp(scores - new_peak[..., None])
    weight_sum = jnp.sum(weights, axis=-1)
    block_values = jnp.einsum(
        "bhqk,bkhd->bhqd",
        weights.astype(jnp.bfloat16),
        value_heads,
        preferred_element_type=jnp.float32,
    )
    return (new_peak, weight_sum, block_values)


def attention_grads(queries, g_att, lse, delta, keys, values, count):
    query_rows, model_width = queries.shape
    key_rows = keys.shape[0]
    query_heads = split_heads(queries)
    grad_heads = split_heads(g_att)
    key_heads = split_heads(keys)
    value_heads = split_heads(values)
    raw_scores = jnp.einsum(
        "qhd,khd->hqk", query_heads, key_heads, preferred_element_type=jnp.float32
    )
    valid_keys = jnp.arange(key_rows, dtype=jnp.int32) < count
    scores = jnp.where(valid_keys[None, None, :], raw_scores * score_scale, masked_value)
    probs = jnp.exp(scores - lse[:, :, None])
    pulled = jnp.einsum("qhd,khd->hqk", grad_heads, value_heads, preferred_element_type=jnp.float32)
    g_scores = (probs * (pulled - delta[:, :, None]) * score_scale).astype(jnp.bfloat16)
    g_queries = jnp.einsum("hqk,khd->qhd", g_scores, key_heads, preferred_element_type=jnp.float32)
    g_keys = jnp.einsum("hqk,qhd->khd", g_scores, query_heads, preferred_element_type=jnp.float32)
    g_values = jnp.einsum(
        "hqk,qhd->khd", probs.astype(jnp.bfloat16), grad_heads, preferred_element_type=jnp.float32
    )
    return (
        g_queries.reshape(query_rows, model_width),
        g_keys.reshape(key_rows, model_width),
        g_values.reshape(key_rows, model_width),
    )


def per_device(
    tokens,
    counts,
    qkv_weight,
    q_bias,
    v_bias,
    out_weight,
    out_bias,
    norm1_gain,
    norm1_bias,
    norm2_gain,
    norm2_bias,
    fc1_weight,
    fc1_bias,
    fc2_weight,
    fc2_bias,
    scale1,
    scale2,
    cotangent,
):
    image_count, local_rows, model_width = tokens.shape
    row_count = image_count * local_rows
    head_width = model_width // HEADS
    scale_first = scale1.astype(jnp.float32)
    scale_second = scale2.astype(jnp.float32)
    inputs = tokens.astype(jnp.float32).reshape(row_count, model_width)
    normed1, norm1_pull = jax.vjp(
        layer_norm, inputs, norm1_gain.astype(jnp.float32), norm1_bias.astype(jnp.float32)
    )
    normed1_low = normed1.astype(jnp.bfloat16)
    projected = jnp.dot(normed1_low, qkv_weight, preferred_element_type=jnp.float32)
    queries = (
        (projected[:, :model_width] + q_bias.astype(jnp.float32))
        .astype(jnp.bfloat16)
        .reshape(image_count, local_rows, model_width)
    )
    keys = (
        projected[:, model_width : 2 * model_width]
        .astype(jnp.bfloat16)
        .reshape(image_count, local_rows, model_width)
    )
    values = (
        (projected[:, 2 * model_width :] + v_bias.astype(jnp.float32))
        .astype(jnp.bfloat16)
        .reshape(image_count, local_rows, model_width)
    )
    carry_start = (
        jnp.full((image_count, HEADS, local_rows), masked_value, jnp.float32),
        jnp.zeros((image_count, HEADS, local_rows), jnp.float32),
        jnp.zeros((image_count, HEADS, local_rows, head_width), jnp.float32),
    )
    fold_step = partial(absorb, split_heads(queries), counts)
    peak_score, weight_sum, weighted = fold_step(
        carry_start,
        (
            lax.all_gather(keys, "blk", axis=1, tiled=True),
            lax.all_gather(values, "blk", axis=1, tiled=True),
        ),
        jnp.int32(0),
    )
    attended_full = weighted / weight_sum[..., None]
    lse = peak_score + jnp.log(weight_sum)
    attended = (
        attended_full.transpose(0, 2, 1, 3).reshape(row_count, model_width).astype(jnp.bfloat16)
    )
    branch = jnp.dot(attended, out_weight, preferred_element_type=jnp.float32) + out_bias.astype(
        jnp.float32
    )
    middle = inputs + scale_first * branch
    normed2, norm2_pull = jax.vjp(
        layer_norm, middle, norm2_gain.astype(jnp.float32), norm2_bias.astype(jnp.float32)
    )
    normed2_low = normed2.astype(jnp.bfloat16)
    hidden_pre = jnp.dot(
        normed2_low, fc1_weight, preferred_element_type=jnp.float32
    ) + fc1_bias.astype(jnp.float32)
    activated, gelu_pull = jax.vjp(gelu_exact, hidden_pre)
    activated_low = activated.astype(jnp.bfloat16)
    mlp_out = jnp.dot(
        activated_low, fc2_weight, preferred_element_type=jnp.float32
    ) + fc2_bias.astype(jnp.float32)
    output = (
        (middle + scale_second * mlp_out)
        .astype(jnp.bfloat16)
        .reshape(image_count, local_rows, model_width)
    )
    g_out = cotangent.astype(jnp.float32).reshape(row_count, model_width)
    grad_scale2 = jnp.sum(g_out * mlp_out, axis=0)
    g_mlp = (scale_second * g_out).astype(jnp.bfloat16)
    grad_fc2_bias = jnp.sum(g_mlp, axis=0, dtype=jnp.float32)
    grad_fc2_weight = left_dot(activated_low, g_mlp)
    g_pre = gelu_pull(right_dot(g_mlp, fc2_weight))[0].astype(jnp.bfloat16)
    grad_fc1_bias = jnp.sum(g_pre, axis=0, dtype=jnp.float32)
    grad_fc1_weight = left_dot(normed2_low, g_pre)
    g_mid_norm, grad_norm2_gain, grad_norm2_bias = norm2_pull(right_dot(g_pre, fc1_weight))
    g_mid = g_out + g_mid_norm
    grad_scale1 = jnp.sum(g_mid * branch, axis=0)
    g_branch = (scale_first * g_mid).astype(jnp.bfloat16)
    grad_out_bias = jnp.sum(g_branch, axis=0, dtype=jnp.float32)
    grad_out_weight = left_dot(attended, g_branch)
    g_att = (
        right_dot(g_branch, out_weight)
        .astype(jnp.bfloat16)
        .reshape(image_count, local_rows, model_width)
    )
    delta = jnp.einsum("brhd,bhrd->bhr", split_heads(g_att).astype(jnp.float32), attended_full)
    key_all, value_all = (
        lax.all_gather(keys, "blk", axis=1, tiled=True),
        lax.all_gather(values, "blk", axis=1, tiled=True),
    )
    g_queries, key_terms, value_terms = lax.map(
        lambda pieces: attention_grads(*pieces),
        (queries, g_att, lse, delta, key_all, value_all, counts),
    )
    g_keys, g_values = (
        lax.psum_scatter(
            key_terms.astype(jnp.bfloat16), "blk", scatter_dimension=1, tiled=True
        ).astype(jnp.float32),
        lax.psum_scatter(
            value_terms.astype(jnp.bfloat16), "blk", scatter_dimension=1, tiled=True
        ).astype(jnp.float32),
    )
    g_queries_low = g_queries.astype(jnp.bfloat16).reshape(row_count, model_width)
    g_keys_low = g_keys.astype(jnp.bfloat16).reshape(row_count, model_width)
    g_values_low = g_values.astype(jnp.bfloat16).reshape(row_count, model_width)
    grad_q_bias = jnp.sum(g_queries_low, axis=0, dtype=jnp.float32)
    grad_v_bias = jnp.sum(g_values_low, axis=0, dtype=jnp.float32)
    g_qkv = jnp.concatenate([g_queries_low, g_keys_low, g_values_low], axis=1)
    grad_qkv_weight = left_dot(normed1_low, g_qkv)
    g_in_norm, grad_norm1_gain, grad_norm1_bias = norm1_pull(right_dot(g_qkv, qkv_weight))
    grad_tokens = (
        (g_mid + g_in_norm).astype(jnp.bfloat16).reshape(image_count, local_rows, model_width)
    )
    summed = (
        lax.psum_scatter(grad_qkv_weight, ("img", "blk"), scatter_dimension=0, tiled=True),
        lax.psum_scatter(grad_q_bias, ("img", "blk"), scatter_dimension=0, tiled=True),
        lax.psum_scatter(grad_v_bias, ("img", "blk"), scatter_dimension=0, tiled=True),
        lax.psum_scatter(grad_out_weight, ("img", "blk"), scatter_dimension=0, tiled=True),
        lax.psum_scatter(grad_out_bias, ("img", "blk"), scatter_dimension=0, tiled=True),
        lax.psum_scatter(grad_norm1_gain, ("img", "blk"), scatter_dimension=0, tiled=True),
        lax.psum_scatter(grad_norm1_bias, ("img", "blk"), scatter_dimension=0, tiled=True),
        lax.psum_scatter(grad_norm2_gain, ("img", "blk"), scatter_dimension=0, tiled=True),
        lax.psum_scatter(grad_norm2_bias, ("img", "blk"), scatter_dimension=0, tiled=True),
        lax.psum_scatter(grad_fc1_weight, ("img", "blk"), scatter_dimension=0, tiled=True),
        lax.psum_scatter(grad_fc1_bias, ("img", "blk"), scatter_dimension=0, tiled=True),
        lax.psum_scatter(grad_fc2_weight, ("img", "blk"), scatter_dimension=0, tiled=True),
        lax.psum_scatter(grad_fc2_bias, ("img", "blk"), scatter_dimension=0, tiled=True),
        lax.psum_scatter(grad_scale1, ("img", "blk"), scatter_dimension=0, tiled=True),
        lax.psum_scatter(grad_scale2, ("img", "blk"), scatter_dimension=0, tiled=True),
    )
    return (
        output,
        grad_tokens,
        summed[0],
        summed[1],
        summed[2],
        summed[3],
        summed[4],
        summed[5],
        summed[6],
        summed[7],
        summed[8],
        summed[9],
        summed[10],
        summed[11],
        summed[12],
        summed[13],
        summed[14],
    )


def solution(mesh):
    in_specs = (
        P("img", "blk", None),
        P("img"),
        P(),
        P(),
        P(),
        P(),
        P(),
        P(),
        P(),
        P(),
        P(),
        P(),
        P(),
        P(),
        P(),
        P(),
        P(),
        P("img", "blk", None),
    )
    out_specs = (
        P("img", "blk", None),
        P("img", "blk", None),
        P(("img", "blk"), None),
        P(("img", "blk")),
        P(("img", "blk")),
        P(("img", "blk"), None),
        P(("img", "blk")),
        P(("img", "blk")),
        P(("img", "blk")),
        P(("img", "blk")),
        P(("img", "blk")),
        P(("img", "blk"), None),
        P(("img", "blk")),
        P(("img", "blk"), None),
        P(("img", "blk")),
        P(("img", "blk")),
        P(("img", "blk")),
    )
    return jax.shard_map(
        per_device, mesh=mesh, in_specs=in_specs, out_specs=out_specs, check_vma=False
    )
```

profile of v0, /device:TPU:0, one launch (start us, length us, event | category | flops | bytes accessed | tf_op | source)
XLA Modules:
  0.0 975.0 jit_solution(7648798244638699292)
XLA Ops:
  41.9 22.3 %all-gather.3.cloned.1.call-done = bf16[3,1024,768]{1,2,0:T(8,128)(2,1)} async-done(((bf16[3,256,768]{1,2,0:T(8,128)(2,1)}), bf16[3,1024,768]{1,2,0:T(8,128)(2,1)}) %all-gather.3.cloned.1.call-update) | async-done | bytes 4718608 | tf_op jit(solution)/shard_map/all_gather | solution.py:148
  64.2 19.4 %fusion.6 = (f32[3,12,256]{2,1,0:T(8,128)S(1)}, f32[3,12,256,1024]{3,2,1,0:T(8,128)}) fusion(pred[3,1024]{1,0:T(4,128)(4,1)S(1)} %iota_compare_fusion.1, bf16[3,1024,12,64]{1,3,2,0:T(8,128)(2,1)} %bitcast.161, bf16[3,256,12,64]{3,2,1,0:T(8,128)(2,1)} %reshape.236), kind=kOutput, calls=%fused_computation.19 | convolution fusion | flops 1236261888 | bytes 43686912 | tf_op jit(solution)/shard_map/bqhd,bkhd->bhqk/dot_general | solution.py:47
  83.6 16.4 %fusion.7 = f32[3,12,256]{2,1,0:T(8,128)S(1)} fusion(f32[3,12,256,1024]{3,2,1,0:T(8,128)} %get-tuple-element.174, f32[3,12,256]{2,1,0:T(8,128)S(1)} %broadcast_maximum_fusion, pred[3,1024]{1,0:T(4,128)(4,1)S(1)} %iota_compare_fusion.1), kind=kLoop, calls=%fused_computation.20 | loop fusion | flops 37739520 | bytes 37825536 | tf_op jit(solution)/shard_map/reduce_sum | solution.py:56
  103.8 17.7 %fusion.23 = (bf16[3,256,12,64]{1,3,2,0:T(8,128)(2,1)S(1)}, f32[3,12,256,64]{2,3,1,0:T(8,128)}) fusion(f32[3,256,12]{1,2,0:T(8,128)} %bitcast.178, bf16[3,1024,12,64]{1,3,2,0:T(8,128)(2,1)} %bitcast.163, f32[3,12,256,1024]{3,2,1,0:T(8,128)} %get-tuple-element.174, f32[3,12,256]{2,1,0:T(8,128)} %copy-done.33, pred[3,1024]{1,0:T(4,128)(4,1)S(1)} %iota_compare_fusion.1), kind=kOutput, calls=%fused_computation.58 | convolution fusion | flops 1246887936 | bytes 46083072 | tf_op jit(solution)/shard_map/bhqk,bkhd->bhqd/dot_general | solution.py:57
  130.6 27.4 %convert_reduce_fusion = (f32[3072]{0:T(1024)}, bf16[768,3072]{1,0:T(8,128)(2,1)S(1)}, f32[768,3072]{1,0:T(8,128)}) fusion(f32[768,3072]{1,0:T(8,128)S(1)} %fusion.46, f32[3072]{0:T(1024)S(1)} %copy-done.34, bf16[768,768]{1,0:T(8,128)(2,1)S(1)} %copy-done.18, bf16[3072,768]{1,0:T(8,128)(2,1)S(1)} %bitcast.182), kind=kOutput, calls=%fused_computation.26 | convolution fusion | flops 3800822784 | bytes 29515776 | tf_op jit(solution)/shard_map/dot_general | solution.py:34
  157.9 4.8 multiply_reduce_fusion.2
  178.0 178.3 %while.14 = (s32[]{:T(128)}, bf16[3,256,768]{2,1,0:T(8,128)(2,1)}, bf16[3,1024,768]{2,1,0:T(8,128)(2,1)}, bf16[3,1024,768]{2,1,0:T(8,128)(2,1)}, bf16[3,1024,768...) while((s32[]{:T(128)}, bf16[3,256,768]{2,1,0:T(8,128)(2,1)}, ...), condition=%wide.region_9.10_spmd, body=%wide.region_8.9_spmd.sunk | while | flops 2047869952 | bytes 124748608 | solution.py:203
  186.2 7.9 fusion.112
  198.7 8.3 multiply_convert_fusion.5
  215.4 7.6 fusion.115
  228.4 5.6 fusion.113
  245.5 7.9 fusion.112
  258.0 8.3 multiply_convert_fusion.5
  274.7 7.6 fusion.115
  287.7 5.6 fusion.113
  304.8 7.9 fusion.112
  317.3 8.3 multiply_convert_fusion.5
  334.0 7.6 fusion.115
  347.0 5.6 fusion.113
  361.8 11.6 %fusion.45 = f32[768,3072]{1,0:T(8,128)} fusion(bf16[768,3072]{1,0:T(8,128)(2,1)} %copy-done.15, f32[768,768]{1,0:T(8,128)} %copy-done.4, f32[768]{0:T(1024)S(1)} %copy-done.32, f32[768]{0:T(1024)S(1)} %copy-done.28, f32[768]{0:T(1024)S(1)} %copy-done.30, f32[768]{0:T(1024)S(1)} %copy-done.26), kind=kOutput, calls=%fused_computation.110 | convolution fusion | flops 3626827776 | bytes 16527360 | tf_op jit(solution)/shard_map/dot_general | solution.py:28
  374.1 11.7 %multiply_convert_fusion.1 = bf16[768,3072]{1,0:T(8,128)(2,1)} fusion(f32[768,3072]{1,0:T(8,128)} %get-tuple-element.156, f32[768,3072]{1,0:T(8,128)} %copy-done.13, f32[3072]{0:T(1024)S(1)} %copy-done.35), kind=kLoop, calls=%fused_computation.28 | loop fusion | flops 9437184 | bytes 23605248 | tf_op jit(solution)/shard_map/convert_element_type | solution.py:170
  385.8 10.2 %fusion.56 = f32[3072,768]{1,0:T(8,128)} fusion(bf16[768,3072]{1,0:T(8,128)(2,1)} %multiply_convert_fusion.1, bf16[768,768]{1,0:T(8,128)(2,1)} %fusion.21), kind=kOutput, calls=%fused_computation.120 | convolution fusion | flops 3623878656 | bytes 15335424 | tf_op jit(solution)/shard_map/dot_general | solution.py:28
  396.3 8.1 reduce-scatter.7.cloned.1.call-done
  404.3 50.4 %reduce-scatter.9.cloned.1.call-done = bf16[3,256,768]{2,1,0:T(8,128)(2,1)} async-done(((bf16[3,1024,768]{2,1,0:T(8,128)(2,1)}), bf16[3,256,768]{2,1,0:T(8,128)(2,1)}) %reduce-scatter.9.cloned.1.call-update) | async-done | bytes 1179664 | tf_op jit(solution)/shard_map/reduce_scatter | solution.py:211
  454.7 8.2 fusion.37
  469.0 5.5 fusion.47
  476.5 6.8 fusion.22
  483.3 41.4 %all-reduce.11 = (f32[768]{0:T(1024)}, f32[768]{0:T(1024)}, f32[768]{0:T(1024)}, f32[768]{0:T(1024)}, f32[768]{0:T(1024)}, /*index=5*/f32[768]{0:T(1024)}, f32[7...) all-reduce(f32[768]{0:T(1024)} %convert_reduce_fusion.5, ...), channel_id=5, replica_groups=mesh['img'=8,'blk'=4] {'img','blk'}, use_global_device_ids=true, to_apply=%region_16.17.clone | all-reduce | flops 10752 | bytes 86016
  537.9 21.7 %reduce-scatter.13.cloned.1.call-done = f32[24,768]{1,0:T(8,128)} async-done(((f32[768,768]{1,0:T(8,128)}), f32[24,768]{1,0:T(8,128)}) %reduce-scatter.13.cloned.1.call-update) | async-done | bytes 73744 | tf_op jit(solution)/shard_map/reduce_scatter | solution.py:230
  559.5 142.0 %reduce-scatter.15.cloned.1.call-done = f32[24,3072]{1,0:T(8,128)} async-done(((f32[768,3072]{1,0:T(8,128)}), f32[24,3072]{1,0:T(8,128)}) %reduce-scatter.15.cloned.1.call-update) | async-done | bytes 294928 | tf_op jit(solution)/shard_map/reduce_scatter | solution.py:236
  701.5 141.1 %reduce-scatter.17.cloned.1.call-done = f32[96,768]{1,0:T(8,128)} async-done(((f32[3072,768]{1,0:T(8,128)}), f32[96,768]{1,0:T(8,128)}) %reduce-scatter.17.cloned.1.call-update) | async-done | bytes 294928 | tf_op jit(solution)/shard_map/reduce_scatter | solution.py:238
  842.6 125.3 %reduce-scatter.11.cloned.1.call-done = f32[24,2304]{1,0:T(8,128)} async-done(((f32[768,2304]{1,0:T(8,128)}), f32[24,2304]{1,0:T(8,128)}) %reduce-scatter.11.cloned.1.call-update) | async-done | bytes 221200 | tf_op jit(solution)/shard_map/reduce_scatter | solution.py:227
  (295 shorter events, 179.4 us)
Async XLA Ops:
  7.2 6.7 copy-start
  7.2 57.0 %all-gather.3.cloned.1.call-start = ((), (), s32[]{:S(2)}) async-start(), calls=%async_computation.6 | async-start | bytes 5898240 | tf_op jit(solution)/shard_map/all_gather | solution.py:148
  23.3 80.6 %all-gather.5.cloned.1.call-start = ((), (), s32[]{:S(2)}) async-start(), calls=%async_computation.7 | async-start | bytes 5898240 | tf_op jit(solution)/shard_map/all_gather | solution.py:149
  30.0 6.6 copy-start.56
  30.0 6.6 copy-start.57
  30.0 374.3 %reduce-scatter.7.cloned.1.call-start = ((), (), s32[]{:S(2)}) async-start(), calls=%async_computation.8 | async-start | bytes 5898240 | tf_op jit(solution)/shard_map/reduce_scatter | solution.py:208
  36.5 126.3 %copy-start.27 = (f32[768]{0:T(1024)}, f32[768]{0:T(1024)S(1)}, u32[]{:S(2)}) copy-start(f32[768]{0:T(1024)S(1)} %convert_element_type.137) | copy-start | bytes 9220
  36.6 89.9 %copy-start.31 = (f32[768]{0:T(1024)}, f32[768]{0:T(1024)S(1)}, u32[]{:S(2)}) copy-start(f32[768]{0:T(1024)S(1)} %convert_element_type.138) | copy-start | bytes 9220
  37.3 46.3 %copy-start.42 = (f32[768]{0:T(1024)}, f32[768]{0:T(1024)S(1)}, u32[]{:S(2)}) copy-start(f32[768]{0:T(1024)S(1)} %convert_element_type.136) | copy-start | bytes 9220
  83.6 16.4 %copy-start.33 = (f32[3,12,256]{2,1,0:T(8,128)}, f32[3,12,256]{2,1,0:T(8,128)S(1)}, u32[]{:S(2)}) copy-start(f32[3,12,256]{2,1,0:T(8,128)S(1)} %broadcast_maximum_fusion) | copy-start | bytes 110596
  123.2 7.3 slice-start.4
  126.0 36.8 %copy-start.4 = (f32[768,768]{1,0:T(8,128)}, f32[768,768]{1,0:T(8,128)S(1)}, u32[]{:S(2)}) copy-start(f32[768,768]{1,0:T(8,128)S(1)} %get-tuple-element.162) | copy-start | bytes 7077892
  126.0 36.8 %copy-start.25 = (f32[768]{0:T(1024)}, f32[768]{0:T(1024)S(1)}, u32[]{:S(2)}) copy-start(f32[768]{0:T(1024)S(1)} %broadcast_multiply_fusion) | copy-start | bytes 9220
  126.5 36.4 %copy-start.29 = (f32[768]{0:T(1024)}, f32[768]{0:T(1024)S(1)}, u32[]{:S(2)}) copy-start(f32[768]{0:T(1024)S(1)} %fusion.39) | copy-start | bytes 9220
  130.5 27.4 %copy-start.13 = (f32[768,3072]{1,0:T(8,128)}, f32[768,3072]{1,0:T(8,128)S(1)}, u32[]{:S(2)}) copy-start(f32[768,3072]{1,0:T(8,128)S(1)} %fusion.46) | copy-start | bytes 28311556
  198.7 8.3 copy-start.60
  198.7 8.3 copy-start.3
  258.0 8.3 copy-start.60
  258.0 8.3 copy-start.3
  317.2 8.3 copy-start.60
  317.3 8.3 copy-start.3
  356.3 98.4 %reduce-scatter.9.cloned.1.call-start = ((), (), s32[]{:S(2)}) async-start(), calls=%async_computation.9 | async-start | bytes 5898240 | tf_op jit(solution)/shard_map/reduce_scatter | solution.py:211
  356.9 202.7 %reduce-scatter.13.cloned.1.call-start = ((), (), s32[]{:S(2)}) async-start(), calls=%async_computation.11 | async-start | bytes 2433024 | tf_op jit(solution)/shard_map/reduce_scatter | solution.py:230
  361.1 340.4 %reduce-scatter.15.cloned.1.call-start = ((), (), s32[]{:S(2)}) async-start(), calls=%async_computation.12 | async-start | bytes 9732096 | tf_op jit(solution)/shard_map/reduce_scatter | solution.py:236
  373.4 469.2 %reduce-scatter.17.cloned.1.call-start = ((), (), s32[]{:S(2)}) async-start(), calls=%async_computation.13 | async-start | bytes 9732096 | tf_op jit(solution)/shard_map/reduce_scatter | solution.py:238
  396.0 572.0 %reduce-scatter.11.cloned.1.call-start = ((), (), s32[]{:S(2)}) async-start(), calls=%async_computation.10 | async-start | bytes 7299072 | tf_op jit(solution)/shard_map/reduce_scatter | solution.py:227
  468.1 8.1 slice-start
  468.1 8.1 slice-start.6
  468.9 7.2 copy-start.12
  468.9 7.2 slice-start.1
  468.9 7.2 slice-start.7
  468.9 7.2 copy-start.62
  (59 other events, 164.5 us)
Sparse Core Ops, SparseCore 0:
  23.4 40.7 all-gather.2
  65.7 38.0 all-gather.4
  356.4 47.8 reduce-scatter.6
  406.9 47.8 reduce-scatter.8
  460.4 99.0 reduce-scatter.12
  566.9 134.5 reduce-scatter.14
  708.0 134.5 reduce-scatter.16
  849.8 118.1 reduce-scatter.10
where the time goes:
time: 981 us; the launch traced here: 975 us
  waiting for transfers between devices  514 us (52%)
  matrix products  224 us (23%)
  local copies, waits for them, and re-layouts  118 us (12%)
  other arithmetic  60.6 us (6%)
  blocking collectives  41.4 us (4%)
  between operations  15.1 us (2%)
    reduce_scatter x1, waiting for transfers between devices, per_device(): lax.psum_scatter(grad_fc1_weight, ('img', 'blk'), scatter_dimension=0, ti...  142 us
    reduce_scatter x1, waiting for transfers between devices, per_device(): lax.psum_scatter(grad_fc2_weight, ('img', 'blk'), scatter_dimension=0, ti...  141 us
    reduce_scatter x1, waiting for transfers between devices, per_device(): lax.psum_scatter(grad_qkv_weight, ('img', 'blk'), scatter_dimension=0, ti...  125 us
    reduce_scatter x1, waiting for transfers between devices, per_device(): lax.psum_scatter(value_terms.astype(jnp.bfloat16), 'blk', scatter_dimensi...  50.4 us
    dynamic_update_slice x18, local copies, waits for them, and re-layouts, per_device(): lax.map(lambda pieces: attention_grads(*pieces), (queries, g_att, lse, de...  43.1 us
    unnamed x1, blocking collectives  41.4 us
    dot_general x4, matrix products, right_dot(): lax.dot_general(left_side, right_side, (((1,), (1,)), ((), ())), preferre...  39.8 us
    dot_general x4, matrix products, left_dot(): lax.dot_general(left_side, right_side, (((0,), (0,)), ((), ())), preferre...  34.2 us
  transfers between devices with their start and end apart: 8, of which 8 were waited for; matrix products, arithmetic and copies ran while one was open for 14% of the time, Pallas kernels for 0%

commit v1 on v0

v1 whole, which is shorter than its diff:
```python
from functools import partial

import jax
import jax.numpy as jnp
from jax import lax
from jax.experimental import pallas as pl
from jax.experimental.pallas import tpu as pltpu
from jax.sharding import PartitionSpec as P

HEADS = 12
WIDTH = 64
score_scale = 0.125
norm_eps = 1e-06
masked_value = -1e30
inv_sqrt2 = 0.7071067811865476
inv_sqrt2pi = 0.3989422804014327
VMEM_LIMIT = 60 * 1024 * 1024
f32 = jnp.float32
bf16 = jnp.bfloat16


def dot_nn(a, b):
    return lax.dot_general(a, b, (((1,), (0,)), ((), ())), preferred_element_type=f32)


def dot_nt(a, b):
    return lax.dot_general(a, b, (((1,), (1,)), ((), ())), preferred_element_type=f32)


def dot_tn(a, b):
    return lax.dot_general(a, b, (((0,), (0,)), ((), ())), preferred_element_type=f32)


def standardize(v):
    average = jnp.mean(v, axis=-1, keepdims=True)
    centered = v - average
    spread = jnp.mean(centered * centered, axis=-1, keepdims=True)
    inverse = lax.rsqrt(spread + norm_eps)
    return centered * inverse, inverse


def params(**kw):
    return pltpu.CompilerParams(vmem_limit_bytes=VMEM_LIMIT, **kw)


def forward_kernel(blocks, nh, rows, info, *refs):
    xs = refs[:blocks]
    vec, w, wb = refs[blocks : blocks + 3]
    n1, qkv, full, lse = refs[blocks + 3 : blocks + 7]
    outs = refs[blocks + 7 : 2 * blocks + 7]
    qs, ks, vt, peak, total, acc = refs[2 * blocks + 7 :]
    hw = nh * WIDTH
    count, me = info[0], info[1]
    gain, shift = vec[0:1, :], vec[1:2, :]
    for m in range(blocks):
        z, _ = standardize(xs[m][...].astype(f32))
        low = (z * gain + shift).astype(bf16)
        n1[m] = low
        proj = (dot_nn(low, w[...]) + wb[...]).astype(bf16)
        qkv[m] = proj
        vt[:, m * rows : (m + 1) * rows] = proj[:, 2 * hw :].T
        for h in range(nh):
            qs[h, m * rows : (m + 1) * rows, :] = proj[:, h * WIDTH : (h + 1) * WIDTH] * score_scale
            ks[h, m * rows : (m + 1) * rows, :] = proj[:, hw + h * WIDTH : hw + (h + 1) * WIDTH]
    peak[...] = jnp.full_like(peak, masked_value)
    total[...] = jnp.zeros_like(total)
    acc[...] = jnp.zeros_like(acc)
    for m in range(blocks):
        valid = count - (me ^ m) * rows

        @pl.when(valid > 0)
        def _():
            keep = lax.broadcasted_iota(jnp.int32, (rows, 1), 0) < valid
            for h in range(nh):
                s = dot_nt(ks[h, m * rows : (m + 1) * rows, :], qs[h])
                s = jnp.where(keep, s, masked_value)
                old = peak[h : h + 1, :]
                new = jnp.maximum(old, jnp.max(s, axis=0, keepdims=True))
                p = jnp.exp(s - new)
                fade = jnp.exp(old - new)
                total[h : h + 1, :] = total[h : h + 1, :] * fade + jnp.sum(p, axis=0, keepdims=True)
                peak[h : h + 1, :] = new
                part = dot_nn(vt[h * WIDTH : (h + 1) * WIDTH, m * rows : (m + 1) * rows], p.astype(bf16))
                acc[h * WIDTH : (h + 1) * WIDTH, :] = acc[h * WIDTH : (h + 1) * WIDTH, :] * fade + part

    lse[...] = jnp.zeros_like(lse)
    for h in range(nh):
        sl = slice(h * WIDTH, (h + 1) * WIDTH)
        lse[h : h + 1, :] = peak[h : h + 1, :] + jnp.log(total[h : h + 1, :])
        done = acc[sl, :] / total[h : h + 1, :]
        full[sl, :] = done
        for m in range(blocks):
            outs[m][sl, :] = done[:, m * rows : (m + 1) * rows].astype(bf16)


def forward_image(info, xs, vec, w, wb, nh):
    blocks = len(xs)
    rows, d = xs[0].shape
    length, hw = rows * blocks, nh * WIDTH
    vm = pl.BlockSpec(memory_space=pltpu.VMEM)
    return pl.pallas_call(
        partial(forward_kernel, blocks, nh, rows),
        name="attend_forward",
        in_specs=[pl.BlockSpec(memory_space=pltpu.SMEM)] + [vm] * (blocks + 3),
        out_specs=[vm] * (4 + blocks),
        out_shape=[
            jax.ShapeDtypeStruct((blocks, rows, d), bf16),
            jax.ShapeDtypeStruct((blocks, rows, 3 * hw), bf16),
            jax.ShapeDtypeStruct((hw, length), f32),
            jax.ShapeDtypeStruct((8, length), f32),
        ]
        + [jax.ShapeDtypeStruct((hw, rows), bf16)] * blocks,
        scratch_shapes=[
            pltpu.VMEM((nh, length, WIDTH), bf16),
            pltpu.VMEM((nh, length, WIDTH), bf16),
            pltpu.VMEM((hw, length), bf16),
            pltpu.VMEM((8, length), f32),
            pltpu.VMEM((8, length), f32),
            pltpu.VMEM((hw, length), f32),
        ],
        compiler_params=params(),
        cost_estimate=pl.CostEstimate(
            flops=2 * length * d * 3 * hw + 8 * length * length * hw, bytes_accessed=8_000_000, transcendentals=0
        ),
    )(info, *xs, vec, w, wb)


def backward_kernel(blocks, nh, rows, info, *refs):
    gats = refs[:blocks]
    n1, qkv, full, lse, w, dw_in, sums_in = refs[blocks : blocks + 7]
    dw, sums, keep_out, pass_out = refs[blocks + 7 : blocks + 11]
    qs, ks, vs, gs, kt, gt, delta, dqt, gall, n1t = refs[blocks + 11 :]
    hw = nh * WIDTH
    length = rows * blocks
    count, me = info[0], info[1]
    for m in range(blocks):
        rs = slice(m * rows, (m + 1) * rows)
        proj = qkv[m]
        kt[:, rs] = proj[:, hw : 2 * hw].T
        g = gats[m][...]
        gt[:, rs] = g
        gr = g.T
        prod = g.astype(f32) * full[:, rs]
        for h in range(nh):
            sl = slice(h * WIDTH, (h + 1) * WIDTH)
            qs[h, rs, :] = proj[:, sl] * score_scale
            ks[h, rs, :] = proj[:, hw + h * WIDTH : hw + (h + 1) * WIDTH]
            vs[h, rs, :] = proj[:, 2 * hw + h * WIDTH : 2 * hw + (h + 1) * WIDTH]
            gs[h, rs, :] = gr[:, sl]
            delta[h : h + 1, rs] = jnp.sum(prod[sl, :], axis=0, keepdims=True)
    dqt[...] = jnp.zeros_like(dqt)
    for m in range(blocks):
        valid = count - (me ^ m) * rows
        rs = slice(m * rows, (m + 1) * rows)

        @pl.when(valid > 0)
        def _():
            keep = lax.broadcasted_iota(jnp.int32, (rows, 1), 0) < valid
            dks, dvs = [], []
            for h in range(nh):
                sl = slice(h * WIDTH, (h + 1) * WIDTH)
                s = dot_nt(ks[h, rs, :], qs[h])
                s = jnp.where(keep, s, masked_value)
                p = jnp.exp(s - lse[h : h + 1, :])
                dp = dot_nn(vs[h, rs, :], gt[sl, :])
                ds = (p * (dp - delta[h : h + 1, :])).astype(bf16)
                dvs.append(dot_nn(p.astype(bf16), gs[h]).astype(bf16))
                dks.append(dot_nn(ds, qs[h]).astype(bf16))
                dqt[sl, :] += dot_nn(kt[sl, rs], ds)
            gall[rs, hw:] = jnp.concatenate(dks + dvs, axis=1)

        @pl.when(valid <= 0)
        def _():
            gall[rs, hw:] = jnp.zeros((rows, 2 * hw), bf16)

    for m in range(blocks):
        rs = slice(m * rows, (m + 1) * rows)
        gall[rs, :hw] = (dqt[:, rs] * score_scale).T.astype(bf16)
        n1t[:, rs] = n1[m].T
    dw[...] = dw_in[...] + dot_nn(n1t[...], gall[...])
    first = jnp.zeros((1, n1.shape[2]), f32)
    second = jnp.zeros((1, n1.shape[2]), f32)
    third = jnp.zeros((1, 3 * hw), f32)
    for m in range(blocks):
        g = gall[m * rows : (m + 1) * rows, :]
        gn = dot_nt(g, w[...])
        first += jnp.sum(gn * n1[m].astype(f32), axis=0, keepdims=True)
        second += jnp.sum(gn, axis=0, keepdims=True)
        third += jnp.sum(g.astype(f32), axis=0, keepdims=True)
        low = gn.astype(bf16)
        if m % 2 == 0:
            keep_out[m // 2] = low
        else:
            pass_out[m // 2] = low
    sums[...] = sums_in[...]
    sums[0:1, :] += first
    sums[1:2, :] += second
    sums[2:3, : 3 * hw] += third


def backward_image(info, gats, n1, qkv, full, lse, w, dw_in, sums_in, nh):
    blocks = len(gats)
    hw, rows = gats[0].shape
    length, d = rows * blocks, n1.shape[2]
    vm = pl.BlockSpec(memory_space=pltpu.VMEM)
    return pl.pallas_call(
        partial(backward_kernel, blocks, nh, rows),
        name="attend_backward",
        in_specs=[pl.BlockSpec(memory_space=pltpu.SMEM)] + [vm] * (blocks + 7),
        out_specs=[vm] * 4,
        out_shape=[
            jax.ShapeDtypeStruct((d, 3 * hw), f32),
            jax.ShapeDtypeStruct((8, d), f32),
            jax.ShapeDtypeStruct((blocks // 2, rows, d), bf16),
            jax.ShapeDtypeStruct((blocks // 2, rows, d), bf16),
        ],
        scratch_shapes=[
            pltpu.VMEM((nh, length, WIDTH), bf16),
            pltpu.VMEM((nh, length, WIDTH), bf16),
            pltpu.VMEM((nh, length, WIDTH), bf16),
            pltpu.VMEM((nh, length, WIDTH), bf16),
            pltpu.VMEM((hw, length), bf16),
            pltpu.VMEM((hw, length), bf16),
            pltpu.VMEM((8, length), f32),
            pltpu.VMEM((hw, length), f32),
            pltpu.VMEM((length, 3 * hw), bf16),
            pltpu.VMEM((d, length), bf16),
        ],
        compiler_params=params(),
        cost_estimate=pl.CostEstimate(
            flops=4 * length * d * 3 * hw + 20 * length * length * hw, bytes_accessed=12_000_000, transcendentals=0
        ),
    )(info, *gats, n1, qkv, full, lse, w, dw_in, sums_in)


def middle_kernel(blocks, images, steps, info, *refs):
    count = blocks * images
    atts = refs[:count]
    x, cot, vec, ow, b1, w1, w2 = refs[count : count + 7]
    out, gmid, dwo, dw1, dw2, gb1, sums = refs[count + 7 : count + 14]
    gats = refs[count + 14 : 2 * count + 14]
    middle, branch, n2, n2t, gm, mlp, gn2 = refs[2 * count + 14 :]
    j = pl.program_id(0)
    me = info[1]
    hw, rows = atts[0].shape
    gain2, shift2, s1, s2 = vec[2:3, :], vec[3:4, :], vec[4:5, :], vec[5:6, :]
    bias_o, bias2 = vec[6:7, :], vec[7:8, :]

    @pl.when(j == 0)
    def _():
        for i in range(images):
            rs = slice(i * rows, (i + 1) * rows)
            total = jnp.zeros((rows, x.shape[1]), f32)
            for m in range(blocks):
                start = pl.multiple_of((me ^ m) * hw, hw)
                total += dot_nn(atts[i * blocks + m][...].T, ow[pl.ds(start, hw), :])
            total = total + bias_o
            branch[rs, :] = total
            mid = x[rs, :].astype(f32) + s1 * total
            middle[rs, :] = mid
            z, _ = standardize(mid)
            low = (z * gain2 + shift2).astype(bf16)
            n2[rs, :] = low
            n2t[:, rs] = low.T
            gm[rs, :] = (s2 * cot[rs, :].astype(f32)).astype(bf16)
        mlp[...] = jnp.zeros_like(mlp)
        gn2[...] = jnp.zeros_like(gn2)

    hp = dot_nn(n2[...], w1[...]) + b1[...]
    phi = 0.5 + 0.5 * lax.erf(hp * inv_sqrt2)
    act = (hp * phi).astype(bf16)
    slope = phi + hp * (jnp.exp(-0.5 * hp * hp) * inv_sqrt2pi)
    mlp[...] += dot_nn(act, w2[...])
    gpre_full = dot_nt(gm[...], w2[...]) * slope
    gpre = gpre_full.astype(bf16)
    dw2[...] = dot_tn(act, gm[...])
    dw1[...] = dot_nn(n2t[...], gpre)
    gb1[...] = jnp.sum(gpre.astype(f32), axis=0, keepdims=True)
    gn2[...] += dot_nt(gpre, w1[...])

    @pl.when(j == steps - 1)
    def _():
        zero = jnp.zeros((1, x.shape[1]), f32)
        g_s2, g_b2, g_gain, g_shift, g_s1, g_bo = zero, zero, zero, zero, zero, zero
        for i in range(images):
            rs = slice(i * rows, (i + 1) * rows)
            mid = middle[rs, :]
            mo = mlp[rs, :] + bias2
            out[rs, :] = (mid + s2 * mo).astype(bf16)
            go = cot[rs, :].astype(f32)
            g_s2 += jnp.sum(go * mo, axis=0, keepdims=True)
            g_b2 += jnp.sum(gm[rs, :].astype(f32), axis=0, keepdims=True)
            g = gn2[rs, :]
            z, inverse = standardize(mid)
            g_gain += jnp.sum(g * z, axis=0, keepdims=True)
            g_shift += jnp.sum(g, axis=0, keepdims=True)
            q = g * gain2
            gmd = go + inverse * (
                q - jnp.mean(q, axis=-1, keepdims=True) - z * jnp.mean(q * z, axis=-1, keepdims=True)
            )
            gmid[rs, :] = gmd
            g_s1 += jnp.sum(gmd * branch[rs, :], axis=0, keepdims=True)
            gb = (s1 * gmd).astype(bf16)
            n2[rs, :] = gb
            g_bo += jnp.sum(gb.astype(f32), axis=0, keepdims=True)
        for m in range(blocks):
            start = pl.multiple_of((me ^ m) * hw, hw)
            term = jnp.zeros((hw, x.shape[1]), f32)
            for i in range(images):
                gb = n2[i * rows : (i + 1) * rows, :]
                term += dot_nn(atts[i * blocks + m][...], gb)
                gats[i * blocks + m][...] = dot_nt(ow[pl.ds(start, hw), :], gb).astype(bf16)
            dwo[pl.ds(start, hw), :] = term
        sums[...] = jnp.concatenate([g_s2, g_b2, g_gain, g_shift, g_s1, g_bo, zero, zero], axis=0)


def middle_layers(info, atts, x, cot, vec, ow, b1, w1, w2, blocks, images):
    hw, rows = atts[0].shape
    total, d = x.shape
    ff = w1.shape[1]
    chunk = 512
    steps = ff // chunk
    whole = lambda shape: pl.BlockSpec(shape, lambda j: (0,) * len(shape))
    return pl.pallas_call(
        partial(middle_kernel, blocks, images, steps),
        name="middle_layers",
        grid=(steps,),
        in_specs=[pl.BlockSpec(memory_space=pltpu.SMEM)]
        + [whole((hw, rows))] * (blocks * images)
        + [
            whole((total, d)),
            whole((total, d)),
            whole(vec.shape),
            whole(ow.shape),
            pl.BlockSpec((1, chunk), lambda j: (0, j)),
            pl.BlockSpec((d, chunk), lambda j: (0, j)),
            pl.BlockSpec((chunk, d), lambda j: (j, 0)),
        ],
        out_specs=[
            whole((total, d)),
            whole((total, d)),
            whole((d, d)),
            pl.BlockSpec((d, chunk), lambda j: (0, j)),
            pl.BlockSpec((chunk, d), lambda j: (j, 0)),
            pl.BlockSpec((1, chunk), lambda j: (0, j)),
            whole((8, d)),
        ]
        + [whole((hw, rows))] * (blocks * images),
        out_shape=[
            jax.ShapeDtypeStruct((total, d), bf16),
            jax.ShapeDtypeStruct((total, d), f32),
            jax.ShapeDtypeStruct((d, d), f32),
            jax.ShapeDtypeStruct((d, ff), f32),
            jax.ShapeDtypeStruct((ff, d), f32),
            jax.ShapeDtypeStruct((1, ff), f32),
            jax.ShapeDtypeStruct((8, d), f32),
        ]
        + [jax.ShapeDtypeStruct((hw, rows), bf16)] * (blocks * images),
        scratch_shapes=[
            pltpu.VMEM((total, d), f32),
            pltpu.VMEM((total, d), f32),
            pltpu.VMEM((total, d), bf16),
            pltpu.VMEM((d, total), bf16),
            pltpu.VMEM((total, d), bf16),
            pltpu.VMEM((total, d), f32),
            pltpu.VMEM((total, d), f32),
        ],
        compiler_params=params(dimension_semantics=("arbitrary",)),
        cost_estimate=pl.CostEstimate(
            flops=12 * total * d * ff + 6 * total * d * d, bytes_accessed=40_000_000, transcendentals=0
        ),
    )(info, *atts, x, cot, vec, ow, b1, w1, w2)


def finish_kernel(x, gmid, gain, *refs):
    out = refs[-1]
    terms = refs[:-1]
    images, rows = x.shape[0], x.shape[1]
    per = len(terms) // images
    for i in range(images):
        z, inverse = standardize(x[i].astype(f32))
        g = sum(terms[i * per + k][0].astype(f32) for k in range(per))
        q = g * gain[...]
        term = inverse * (q - jnp.mean(q, axis=-1, keepdims=True) - z * jnp.mean(q * z, axis=-1, keepdims=True))
        out[i] = (gmid[i * rows : (i + 1) * rows, :] + term).astype(bf16)


def finish(x, gmid, gain, terms):
    rows, d = x.shape[1:]
    images = x.shape[0]
    vm = pl.BlockSpec(memory_space=pltpu.VMEM)
    head = pl.BlockSpec((1, rows, d), lambda i: (0, 0, 0))
    return pl.pallas_call(
        finish_kernel,
        name="finish_tokens",
        grid=(1,),
        in_specs=[vm, vm, vm] + [head] * len(terms),
        out_specs=vm,
        out_shape=jax.ShapeDtypeStruct(x.shape, bf16),
        compiler_params=params(),
    )(x, gmid, gain, *terms)


class Places:
    def __init__(self, mesh):
        self.n_img, self.n_blk = mesh.shape["img"], mesh.shape["blk"]
        self.img_bits = self.n_img.bit_length() - 1
        self.blk_bits = self.n_blk.bit_length() - 1
        self.img, self.blk = lax.axis_index("img"), lax.axis_index("blk")
        self.dims = [("img", k) for k in reversed(range(self.img_bits))] + [
            ("blk", k) for k in reversed(range(self.blk_bits))
        ]

    def bit(self, dim):
        axis, k = dim
        return ((self.img if axis == "img" else self.blk) >> k) & 1

    def swap(self, value, dim):
        axis, k = dim
        n = self.n_img if axis == "img" else self.n_blk
        return lax.ppermute(value, axis, [(i, i ^ (1 << k)) for i in range(n)])


def scatter_sum(places, own, dims, order, link=bf16):
    body = own.shape[1:]
    terms = [(own.reshape((2,) * len(dims) + body), list(dims))]
    known = {}

    def part(term, extra):
        value, has = term
        starts = [extra[d] if d in extra else 0 for d in has] + [0] * len(body)
        sizes = [1 if d in extra else 2 for d in has] + list(body)
        left = [2 for d in has if d not in extra]
        return lax.dynamic_slice(value, starts, sizes).reshape(tuple(left) + body).astype(f32)

    def add(extra):
        total = part(terms[0], extra)
        for term in terms[1:]:
            total = total + part(term, extra)
        return total

    for dim in order:
        bit = places.bit(dim)
        send = add({**known, dim: 1 - bit}).astype(link)
        known[dim] = bit
        terms.append((places.swap(send, dim), [d for d in dims if d not in known]))
    return add(known)


def solution(mesh):
    def per_device(
        tokens,
        counts,
        qkv_weight,
        q_bias,
        v_bias,
        out_weight,
        out_bias,
        norm1_gain,
        norm1_bias,
        norm2_gain,
        norm2_bias,
        fc1_weight,
        fc1_bias,
        fc2_weight,
        fc2_bias,
        scale1,
        scale2,
        cotangent,
    ):
        places = Places(mesh)
        images, rows, d = tokens.shape
        blocks = places.n_blk
        nh = HEADS // blocks
        hw = nh * WIDTH
        total = images * rows
        me = places.blk
        vec = jnp.stack(
            [norm1_gain, norm1_bias, norm2_gain, norm2_bias, scale1, scale2, out_bias, fc2_bias]
        ).astype(f32)
        w = jnp.concatenate(
            [lax.dynamic_slice(qkv_weight, (0, k * d + me * hw), (d, hw)) for k in range(3)], axis=1
        )
        wb = jnp.concatenate(
            [
                lax.dynamic_slice(q_bias, (me * hw,), (hw,)),
                jnp.zeros((hw,), bf16),
                lax.dynamic_slice(v_bias, (me * hw,), (hw,)),
            ]
        ).astype(f32)[None, :]
        infos = [jnp.stack([counts[i], me.astype(jnp.int32)]) for i in range(images)]

        def swap_blk(value, m):
            return lax.ppermute(value, "blk", [(b, b ^ m) for b in range(blocks)])

        saved, atts = [], []
        for i in range(images):
            found = {0: tokens[i]}
            for k in reversed(range(places.blk_bits)):
                found.update({m | 1 << k: swap_blk(v, 1 << k) for m, v in found.items()})
            xs = [found[m] for m in range(blocks)]
            n1, qkv, full, lse, *outs = forward_image(infos[i], xs, vec, w, wb, nh)
            saved.append((n1, qkv, full, lse))
            atts.extend([outs[0]] + [swap_blk(outs[m], m) for m in range(1, blocks)])
        out, gmid, dwo, dw1, dw2, gb1, sums, *gats = middle_layers(
            infos[0],
            atts,
            tokens.reshape(total, d),
            cotangent.reshape(total, d),
            vec,
            out_weight,
            fc1_bias.astype(f32)[None, :],
            fc1_weight,
            fc2_weight,
            blocks,
            images,
        )
        n = places.n_img * blocks
        share = d // n
        ff = fc1_weight.shape[1]
        z_dims = [("img", k) for k in range(places.img_bits)]
        core, far_x = ("blk", 0), ("blk", 1)
        order_y = [core] + z_dims + [far_x]
        order_x = [core, far_x] + z_dims
        grad_fc2 = scatter_sum(places, dw2.reshape(n, ff // n, d), places.dims, order_x)
        grad_fc1 = scatter_sum(places, dw1.reshape(n, share, ff), places.dims, order_y)
        grad_out = scatter_sum(places, dwo.reshape(n, share, d), places.dims, order_y)

        dw = jnp.zeros((d, 3 * hw), f32)
        sums1 = jnp.zeros((8, d), f32)
        terms = []
        for i in range(images):
            pieces = [gats[i * blocks]] + [swap_blk(gats[i * blocks + m], m) for m in range(1, blocks)]
            dw, sums1, kept, passed = backward_image(infos[i], pieces, *saved[i], w, dw, sums1, nh)
            near = swap_blk(passed, 1)
            step = (kept[1].astype(f32) + near[1].astype(f32)).astype(bf16)[None]
            terms.extend([kept, near, swap_blk(step, 2)])
        grad_tokens = finish(tokens, gmid, vec[0:1, :], terms)

        img_dims = [("img", k) for k in reversed(range(places.img_bits))]
        part = scatter_sum(places, dw.reshape(places.n_img, blocks * share, 3 * hw), img_dims, z_dims)
        part = part.reshape(blocks, share, 3 * hw)
        pieces = [
            lax.dynamic_slice(part, (me ^ m, 0, 0), (1, share, 3 * hw))[0].astype(bf16) for m in range(blocks)
        ]
        pieces = jnp.stack([pieces[0]] + [swap_blk(pieces[m], m) for m in range(1, blocks)])
        by_source = [lax.dynamic_slice(pieces, (me ^ b, 0, 0), (1, share, 3 * hw))[0] for b in range(blocks)]
        grad_qkv = jnp.concatenate(
            [by_source[b][:, k * hw : (k + 1) * hw] for k in range(3) for b in range(blocks)], axis=1
        ).astype(f32)

        placed = lambda v: lax.dynamic_update_slice(jnp.zeros((d,), f32), v, (me * hw,))
        g_n1b = sums1[1]
        g_n1g = (sums1[0] - vec[1] * sums1[1]) / vec[0]
        g_qb, g_vb = placed(sums1[2, :hw]), placed(sums1[2, 2 * hw : 3 * hw])
        g_s2, g_b2, g_n2g, g_n2b, g_s1, g_bo = [sums[k] for k in range(6)]
        small = jnp.stack([g_qb, g_vb, g_bo, g_n1g, g_n1b, g_n2g, g_n2b, g_b2, g_s1, g_s2])
        small = small.reshape(10, n, share).transpose(1, 0, 2).reshape(n, 1, 10 * share)
        small = jnp.concatenate([small, gb1.reshape(n, 1, ff // n)], axis=2)
        small = scatter_sum(places, small, places.dims, order_y, link=f32)[0]
        v = [small[k * share : (k + 1) * share] for k in range(10)]
        g_b1 = small[10 * share :]
        return (
            out.reshape(images, rows, d),
            grad_tokens,
            grad_qkv,
            v[0],
            v[1],
            grad_out,
            v[2],
            v[3],
            v[4],
            v[5],
            v[6],
            grad_fc1,
            g_b1,
            grad_fc2,
            v[7],
            v[8],
            v[9],
        )

    both = P(("img", "blk"))
    both2 = P(("img", "blk"), None)
    rows_spec = P("img", "blk", None)
    in_specs = (rows_spec, P("img")) + (P(),) * 15 + (rows_spec,)
    out_specs = (
        rows_spec,
        rows_spec,
        both2,
        both,
        both,
        both2,
        both,
        both,
        both,
        both,
        both,
        both2,
        both,
        both2,
        both,
        both,
        both,
    )
    return jax.shard_map(per_device, mesh=mesh, in_specs=in_specs, out_specs=out_specs, check_vma=False)
```

time: 981 us -> 347 us (0.35)
  waiting for transfers between devices: 514 us -> 73.3 us
  matrix products: 224 us -> 0 us
  Pallas kernels: 0 us -> 126 us
  local copies, waits for them, and re-layouts: 118 us -> 29.9 us
  starting transfers between devices: 1.24 us -> 75.8 us
  blocking collectives: 41.4 us -> 0 us
  other arithmetic: 60.6 us -> 38.8 us
  between operations: 15.1 us -> 2.08 us
    reduce_scatter x6 -> x0, waiting for transfers between devices: 489 us -> none  [the longest x1 142 us: per_device(): lax.psum_scatter(grad_fc1_weight, ('img', 'blk'), scatter_dimension=0, ti...]
    dot_general x29 -> x0, matrix products: 224 us -> none  [the longest x4 39.8 us: right_dot(): lax.dot_general(left_side, right_side, (((1,), (1,)), ((), ())), preferre...]
    pallas_call x0 -> x8, Pallas kernels: none -> 126 us  [the longest x3 41.2 us: backward_image(): pl.pallas_call(partial(backward_kernel, blocks, nh, rows), name='attend_b...]
    ppermute x0 -> x59, starting transfers between devices: none -> 75.8 us  [the longest x23 52.6 us: swap(): return lax.ppermute(value, axis, [(i, i ^ 1 << k) for i in range(n)])]
    ppermute x0 -> x59, waiting for transfers between devices: none -> 73.3 us  [the longest x36 38.3 us: swap_blk(): return lax.ppermute(value, 'blk', [(b, b ^ m) for b in range(blocks)])]
    dynamic_update_slice x18 -> x2, local copies, waits for them, and re-layouts: 43.1 us -> 0.33 us  [per_device(): lax.dynamic_update_slice(jnp.zeros((d,), f32), v, (me * hw,))]
    unnamed x1 -> x0, blocking collectives: 41.4 us -> none
    dynamic_slice x15 -> x3, local copies, waits for them, and re-layouts: 33 us -> 3.48 us  [the longest x1 1.97 us: per_device(): lax.dynamic_slice(qkv_weight, (0, k * d + me * hw), (d, hw))]
  transfers between devices with their start and end apart: 8 -> 59, of which waited for: 8 -> 18; matrix products, arithmetic and copies ran while one was open for 14% -> 17% of each run, Pallas kernels for 0% -> 25%
where the time goes in v1:
time: 347 us; the launch traced here: 346 us
  Pallas kernels  126 us (36%)
  starting transfers between devices  75.8 us (22%)
  waiting for transfers between devices  73.3 us (21%)
  other arithmetic  38.8 us (11%)
  local copies, waits for them, and re-layouts  29.9 us (9%)
    ppermute x23, starting transfers between devices, swap(): return lax.ppermute(value, axis, [(i, i ^ 1 << k) for i in range(n)])  52.6 us
    pallas_call x3, Pallas kernels, backward_image(): pl.pallas_call(partial(backward_kernel, blocks, nh, rows), name='attend_b...  41.2 us
    pallas_call x1, Pallas kernels, middle_layers(): pl.pallas_call(partial(middle_kernel, blocks, images, steps), name='middl...  39.8 us
    pallas_call x3, Pallas kernels, forward_image(): pl.pallas_call(partial(forward_kernel, blocks, nh, rows), name='attend_fo...  39.5 us
    ppermute x36, waiting for transfers between devices, swap_blk(): return lax.ppermute(value, 'blk', [(b, b ^ m) for b in range(blocks)])  38.3 us
    ppermute x23, waiting for transfers between devices, swap(): return lax.ppermute(value, axis, [(i, i ^ 1 << k) for i in range(n)])  35 us
    ppermute x36, starting transfers between devices, swap_blk(): return lax.ppermute(value, 'blk', [(b, b ^ m) for b in range(blocks)])  23.3 us
    convert_element_type x14, other arithmetic, scatter_sum(): send = add({**known, dim: 1 - bit}).astype(link)  20 us
  transfers between devices with their start and end apart: 59, of which 18 were waited for; matrix products, arithmetic and copies ran while one was open for 17% of the time, Pallas kernels for 25%

profile of v1, /device:TPU:0, one launch (start us, length us, event | category | flops | bytes accessed | tf_op | source)
XLA Modules:
  0.0 346.3 jit_solution(6270666264137558104)
XLA Ops:
  2.1 3.0 collective-permute-start.13
  11.4 3.8 %collective-permute-done.13.refs_2_ = bf16[256,768]{1,0:T(8,128)(2,1)} collective-permute-done((bf16[256,768]{1,0:T(8,128)(2,1)S(1)}, bf16[256,768]{1,0:T(8,128)(2,1)}, u32[]{:S(2)}, u32[]{:S(2)}) %collective-permute-start.13) | collective-permute-done | bytes 393248 | tf_op jit(solution)/shard_map/ppermute | solution.py:494
  18.4 5.1 %collective-permute-done.7.refs_2_ = bf16[256,768]{1,0:T(8,128)(2,1)S(1)} collective-permute-done((bf16[256,768]{1,0:T(8,128)(2,1)S(1)}, bf16[256,768]{1,0:T(8,128)(2,1)S(1)}, u32[]{:S(2)}, u32[]{:S(2)}) %collective-permute-start.7) | collective-permute-done | bytes 393248 | tf_op jit(solution)/shard_map/ppermute | solution.py:494
  27.4 3.7 %collective-permute-done.1.refs_2_ = bf16[256,768]{1,0:T(8,128)(2,1)S(1)} collective-permute-done((bf16[256,768]{1,0:T(8,128)(2,1)S(1)}, bf16[256,768]{1,0:T(8,128)(2,1)S(1)}, u32[]{:S(2)}, u32[]{:S(2)}) %collective-permute-start.1) | collective-permute-done | bytes 393248 | tf_op jit(solution)/shard_map/ppermute | solution.py:494
  31.1 13.7 %attend_forward.5 = (bf16[4,256,768]{2,1,0:T(8,128)(2,1)}, bf16[4,256,576]{2,1,0:T(8,128)(2,1)}, f32[192,1024]{1,0:T(8,128)}, f32[8,1024]{1,0:T(8,128)}, bf16[19...) custom-call(s32[2]{0:T(128)} %pad_add_fusion.2.info, ...), custom_call_target="tpu_custom_call" | custom-call | flops 2516582400 | bytes 8000000 | tf_op jit(solution)/shard_map/attend_forward/pallas_call | solution.py:101
  47.1 7.6 %attend_forward.4 = (bf16[4,256,768]{2,1,0:T(8,128)(2,1)}, bf16[4,256,576]{2,1,0:T(8,128)(2,1)}, f32[192,1024]{1,0:T(8,128)}, f32[8,1024]{1,0:T(8,128)}, bf16[19...) custom-call(s32[2]{0:T(128)} %pad_add_fusion.1.info, ...), custom_call_target="tpu_custom_call" | custom-call | flops 2516582400 | bytes 8000000 | tf_op jit(solution)/shard_map/attend_forward/pallas_call | solution.py:101
  57.0 18.1 %attend_forward.3 = (bf16[4,256,768]{2,1,0:T(8,128)(2,1)}, bf16[4,256,576]{2,1,0:T(8,128)(2,1)}, f32[192,1024]{1,0:T(8,128)}, f32[8,1024]{1,0:T(8,128)}, bf16[19...) custom-call(s32[2]{0:T(128)} %pad_add_fusion.info, ...), custom_call_target="tpu_custom_call" | custom-call | flops 2516582400 | bytes 8000000 | tf_op jit(solution)/shard_map/attend_forward/pallas_call | solution.py:101
  78.1 3.5 %collective-permute-done.4.refs_2_ = bf16[192,256]{1,0:T(8,128)(2,1)S(1)} collective-permute-done((bf16[192,256]{1,0:T(8,128)(2,1)}, bf16[192,256]{1,0:T(8,128)(2,1)S(1)}, u32[]{:S(2)}, u32[]{:S(2)}) %collective-permute-start.4) | collective-permute-done | bytes 98336 | tf_op jit(solution)/shard_map/ppermute | solution.py:494
  83.2 39.8 %middle_layers.1 = (bf16[768,768]{1,0:T(8,128)(2,1)}, f32[768,768]{1,0:T(8,128)}, f32[768,768]{1,0:T(8,128)}, f32[768,3072]{1,0:T(8,128)}, f32[3072,768]{1,0:T(8...) custom-call(s32[2]{0:T(128)} %pad_add_fusion.info, ...), custom_call_target="tpu_custom_call" | custom-call | flops 24461180928 | bytes 40000000 | tf_op jit(solution)/shard_map/middle_layers/pallas_call | solution.py:324
  123.1 4.1 %fusion = bf16[2,2,2,2,96,768]{5,4,0,3,2,1:T(8,128)(2,1)} fusion(f32[2,2,2,2,2,96,768]{6,5,4,3,2,1,0:T(8,128)} %bitcast.369, s32[]{:T(128)S(6)} %select_n.52), kind=kLoop, calls=%fused_computation.2 | loop fusion | bytes 4718596 | tf_op jit(solution)/shard_map/convert_element_type | solution.py:444
  127.6 4.2 %fusion.1 = bf16[2,2,2,2,24,3072]{5,4,3,2,1,0:T(8,128)(2,1)} fusion(f32[2,2,2,2,2,24,3072]{6,5,4,3,2,1,0:T(8,128)} %bitcast.363, s32[]{:T(128)S(6)} %select_n.52), kind=kLoop, calls=%fused_computation.3 | loop fusion | bytes 4718596 | tf_op jit(solution)/shard_map/convert_element_type | solution.py:444
  141.8 13.2 %attend_backward.3 = (f32[768,576]{1,0:T(8,128)}, f32[8,768]{1,0:T(8,128)}, bf16[2,256,768]{2,1,0:T(8,128)(2,1)}, bf16[2,256,768]{2,1,0:T(8,128)(2,1)}) custom-call(s32[2]{0:T(128)} %pad_add_fusion.info, bf16[192,256]{1,0:T(8,128)(2,1)} %get-tuple-element.86.refs_0_, bf16[192,256]{1,0:T(8,128)(2,1)} %copy-done.50, bf16[192,256]{1,0:T(8,128)(2,1)} %copy-done.52, ...), custom_call_target="tpu_custom_call" | custom-call | flops 5838471168 | bytes 12000000 | tf_op jit(solution)/shard_map/attend_backward/pallas_call | solution.py:206
  157.4 10.7 %attend_backward.4 = (f32[768,576]{1,0:T(8,128)}, f32[8,768]{1,0:T(8,128)}, bf16[2,256,768]{2,1,0:T(8,128)(2,1)}, bf16[2,256,768]{2,1,0:T(8,128)(2,1)}) custom-call(s32[2]{0:T(128)} %pad_add_fusion.1.info, bf16[192,256]{1,0:T(8,128)(2,1)} %get-tuple-element.96.refs_0_, bf16[192,256]{1,0:T(8,128)(2,1)} %copy-done.49, bf16[192,256]{1,0:T(8,128)(2,1)} %copy-done.54, ...), custom_call_target="tpu_custom_call" | custom-call | flops 5838471168 | bytes 12000000 | tf_op jit(solution)/shard_map/attend_backward/pallas_call | solution.py:206
  168.7 17.3 %attend_backward.5 = (f32[768,576]{1,0:T(8,128)}, f32[8,768]{1,0:T(8,128)}, bf16[2,256,768]{2,1,0:T(8,128)(2,1)}, bf16[2,256,768]{2,1,0:T(8,128)(2,1)}) custom-call(s32[2]{0:T(128)} %pad_add_fusion.2.info, bf16[192,256]{1,0:T(8,128)(2,1)} %get-tuple-element.108.refs_0_, bf16[192,256]{1,0:T(8,128)(2,1)} %copy-done.56, bf16[192,256]{1,0:T(8,128)(2,1)} %copy-done.58, ...), custom_call_target="tpu_custom_call" | custom-call | flops 5838471168 | bytes 12000000 | tf_op jit(solution)/shard_map/attend_backward/pallas_call | solution.py:206
  192.0 2.2 collective-permute-done.40
  194.3 21.6 %collective-permute-start.41 = (f32[2,2,1,336]{3,2,1,0:T(1,128)S(1)}, f32[2,2,1,336]{3,2,1,0:T(1,128)S(1)}, u32[]{:S(2)}, u32[]{:S(2)}) collective-permute-start(f32[2,2,1,336]{3,2,1,0:T(1,128)S(1)} %fusion.33), channel_id=1, source_target_pairs={{0,8},{4,12},{8,0},{12,4},{16,24},{20,28},{24,16},{28,20},{1,9},{5... | collective-permute-start | bytes 16136 | tf_op jit(solution)/shard_map/ppermute | solution.py:421
  219.1 3.0 collective-permute-done.42
  224.6 2.1 collective-permute-start.33
  227.4 7.9 %collective-permute-done.33 = bf16[2,2,96,576]{3,2,1,0:T(8,128)(2,1)S(1)} collective-permute-done((bf16[2,2,96,576]{3,2,1,0:T(8,128)(2,1)S(1)}, bf16[2,2,96,576]{3,2,1,0:T(8,128)(2,1)S(1)}, u32[]{:S(2)}, u32[]{:S(2)}) %collective-permute-start.33) | collective-permute-done | bytes 442400 | tf_op jit(solution)/shard_map/ppermute | solution.py:421
  238.1 3.6 %collective-permute-done.34 = bf16[2,96,576]{2,1,0:T(8,128)(2,1)S(1)} collective-permute-done((bf16[2,96,576]{2,1,0:T(8,128)(2,1)S(1)}, bf16[2,96,576]{2,1,0:T(8,128)(2,1)S(1)}, u32[]{:S(2)}, u32[]{:S(2)}) %collective-permute-start.34) | collective-permute-done | bytes 221216 | tf_op jit(solution)/shard_map/ppermute | solution.py:421
  241.7 4.6 %collective-permute-start.35 = (bf16[96,576]{1,0:T(8,128)(2,1)S(1)}, bf16[96,576]{1,0:T(8,128)(2,1)S(1)}, u32[]{:S(2)}, u32[]{:S(2)}) collective-permute-start(bf16[96,576]{1,0:T(8,128)(2,1)S(1)} %fusion.17), channel_id=1, source_target_pairs={{0,16},{4,20},{8,24},{12,28},{16,0},{20,4},{24,8},{28,12},{1,17},{... | collective-permute-start | bytes 331784 | tf_op jit(solution)/shard_map/ppermute | solution.py:421
  247.4 5.5 %collective-permute-done.35 = bf16[96,576]{1,0:T(8,128)(2,1)S(1)} collective-permute-done((bf16[96,576]{1,0:T(8,128)(2,1)S(1)}, bf16[96,576]{1,0:T(8,128)(2,1)S(1)}, u32[]{:S(2)}, u32[]{:S(2)}) %collective-permute-start.35) | collective-permute-done | bytes 110624 | tf_op jit(solution)/shard_map/ppermute | solution.py:421
  254.5 2.3 fusion.2
  266.9 19.2 %collective-permute-done.37 = bf16[24,576]{1,0:T(8,128)(2,1)S(1)} collective-permute-done((bf16[24,576]{1,0:T(8,128)(2,1)S(1)}, bf16[24,576]{1,0:T(8,128)(2,1)S(1)}, u32[]{:S(2)}, u32[]{:S(2)}) %collective-permute-start.37) | collective-permute-done | bytes 27680 | tf_op jit(solution)/shard_map/ppermute | solution.py:494
  288.2 2.1 fusion.4
  291.9 2.3 fusion.5
  297.2 3.4 collective-permute-start.47
  304.5 3.7 %collective-permute-done.47 = bf16[2,24,768]{2,1,0:T(8,128)(2,1)} collective-permute-done((bf16[2,24,768]{2,1,0:T(8,128)(2,1)}, bf16[2,24,768]{2,1,0:T(8,128)(2,1)}, u32[]{:S(2)}, u32[]{:S(2)}) %collective-permute-start.47) | collective-permute-done | bytes 73760 | tf_op jit(solution)/shard_map/ppermute | solution.py:421
  311.3 2.2 fusion.7
  313.5 4.1 %collective-permute-start.57 = (bf16[2,96,768]{2,1,0:T(8,128)(2,1)}, bf16[2,96,768]{2,1,0:T(8,128)(2,1)}, u32[]{:S(2)}, u32[]{:S(2)}) collective-permute-start(bf16[2,96,768]{2,1,0:T(8,128)(2,1)} %fusion.7), channel_id=1, source_target_pairs={{0,8},{4,12},{8,0},{12,4},{16,24},{20,28},{24,16},{28,20},{1,9},{5... | collective-permute-start | bytes 884744 | tf_op jit(solution)/shard_map/ppermute | solution.py:421
  323.4 5.8 %finish_tokens.1 = bf16[3,256,768]{2,1,0:T(8,128)(2,1)} custom-call(bf16[3,256,768]{2,1,0:T(8,128)(2,1)} %x.1, f32[768,768]{1,0:T(8,128)} %get-tuple-element.85.gmid, f32[1,768]{1,0:T(1,128)} %slice.232.gain, bf16[2,256,768]{2,1,0:T(8,128)(2,1)} %get-tuple-element.94.refs_0_, bf16[2,256,768]{2,1,0:T(8,128)(2,1)} %copy-done.5, ...), custom_call_target="tpu_custom_call" | custom-call | tf_op jit(solution)/shard_map/finish_tokens/pallas_call | solution.py:393
  332.0 5.7 %collective-permute-done.52 = bf16[2,24,3072]{2,1,0:T(8,128)(2,1)} collective-permute-done((bf16[2,24,3072]{2,1,0:T(8,128)(2,1)}, bf16[2,24,3072]{2,1,0:T(8,128)(2,1)}, u32[]{:S(2)}, u32[]{:S(2)}) %collective-permute-start.52) | collective-permute-done | bytes 294944 | tf_op jit(solution)/shard_map/ppermute | solution.py:421
  (317 shorter events, 95.2 us)
Async XLA Ops:
  5.1 21.7 %collective-permute-start.12 = (bf16[256,768]{1,0:T(8,128)(2,1)S(1)}, bf16[256,768]{1,0:T(8,128)(2,1)}, u32[]{:S(2)}, u32[]{:S(2)}) collective-permute-start(bf16[256,768]{1,0:T(8,128)(2,1)S(1)} %get-tuple-element.136.refs_0_), channel_id=1, source_target_pairs={{0,1},{1,0},{2,3},{3,2},{4,5},{5,4},{6,7},{7,6},{8,9},{9,8},{10,11... | collective-permute-start | bytes 1179656 | tf_op jit(solution)/shard_map/ppermute | solution.py:494
  5.2 18.4 %collective-permute-start.7 = (bf16[256,768]{1,0:T(8,128)(2,1)S(1)}, bf16[256,768]{1,0:T(8,128)(2,1)S(1)}, u32[]{:S(2)}, u32[]{:S(2)}) collective-permute-start(bf16[256,768]{1,0:T(8,128)(2,1)S(1)} %get-tuple-element.137.refs_0_), channel_id=1, source_target_pairs={{0,2},{1,3},{2,0},{3,1},{4,6},{5,7},{6,4},{7,5},{8,10},{9,11},{10,... | collective-permute-start | bytes 1179656 | tf_op jit(solution)/shard_map/ppermute | solution.py:494
  5.3 40.0 %collective-permute-start.6 = (bf16[256,768]{1,0:T(8,128)(2,1)S(1)}, bf16[256,768]{1,0:T(8,128)(2,1)}, u32[]{:S(2)}, u32[]{:S(2)}) collective-permute-start(bf16[256,768]{1,0:T(8,128)(2,1)S(1)} %get-tuple-element.137.refs_0_), channel_id=1, source_target_pairs={{0,1},{1,0},{2,3},{3,2},{4,5},{5,4},{6,7},{7,6},{8,9},{9,8},{10,11... | collective-permute-start | bytes 1179656 | tf_op jit(solution)/shard_map/ppermute | solution.py:494
  5.7 25.5 %collective-permute-start.1 = (bf16[256,768]{1,0:T(8,128)(2,1)S(1)}, bf16[256,768]{1,0:T(8,128)(2,1)S(1)}, u32[]{:S(2)}, u32[]{:S(2)}) collective-permute-start(bf16[256,768]{1,0:T(8,128)(2,1)S(1)} %get-tuple-element.138.refs_0_), channel_id=1, source_target_pairs={{0,2},{1,3},{2,0},{3,1},{4,6},{5,7},{6,4},{7,5},{8,10},{9,11},{10,... | collective-permute-start | bytes 1179656 | tf_op jit(solution)/shard_map/ppermute | solution.py:494
  15.2 15.9 %collective-permute-start.14 = (bf16[256,768]{1,0:T(8,128)(2,1)}, bf16[256,768]{1,0:T(8,128)(2,1)}, u32[]{:S(2)}, u32[]{:S(2)}) collective-permute-start(bf16[256,768]{1,0:T(8,128)(2,1)} %collective-permute-done.13.refs_2_), channel_id=1, source_target_pairs={{0,1},{1,0},{2,3},{3,2},{4,5},{5,4},{6,7},{7,6},{8,9},{9,8},{10,11... | collective-permute-start | bytes 1179656 | tf_op jit(solution)/shard_map/ppermute | solution.py:494
  23.5 23.6 %collective-permute-start.8 = (bf16[256,768]{1,0:T(8,128)(2,1)S(1)}, bf16[256,768]{1,0:T(8,128)(2,1)}, u32[]{:S(2)}, u32[]{:S(2)}) collective-permute-start(bf16[256,768]{1,0:T(8,128)(2,1)S(1)} %collective-permute-done.7.refs_2_), channel_id=1, source_target_pairs={{0,1},{1,0},{2,3},{3,2},{4,5},{5,4},{6,7},{7,6},{8,9},{9,8},{10,11... | collective-permute-start | bytes 1179656 | tf_op jit(solution)/shard_map/ppermute | solution.py:494
  26.9 27.8 %collective-permute-start = (bf16[256,768]{1,0:T(8,128)(2,1)S(1)}, bf16[256,768]{1,0:T(8,128)(2,1)S(1)}, u32[]{:S(2)}, u32[]{:S(2)}) collective-permute-start(bf16[256,768]{1,0:T(8,128)(2,1)S(1)} %get-tuple-element.138.refs_0_), channel_id=1, source_target_pairs={{0,1},{1,0},{2,3},{3,2},{4,5},{5,4},{6,7},{7,6},{8,9},{9,8},{10,11... | collective-permute-start | bytes 1179656 | tf_op jit(solution)/shard_map/ppermute | solution.py:494
  31.1 25.2 %collective-permute-start.2 = (bf16[256,768]{1,0:T(8,128)(2,1)S(1)}, bf16[256,768]{1,0:T(8,128)(2,1)S(1)}, u32[]{:S(2)}, u32[]{:S(2)}) collective-permute-start(bf16[256,768]{1,0:T(8,128)(2,1)S(1)} %collective-permute-done.1.refs_2_), channel_id=1, source_target_pairs={{0,1},{1,0},{2,3},{3,2},{4,5},{5,4},{6,7},{7,6},{8,9},{9,8},{10,11... | collective-permute-start | bytes 1179656 | tf_op jit(solution)/shard_map/ppermute | solution.py:494
  44.9 30.3 %collective-permute-start.15 = (bf16[192,256]{1,0:T(8,128)(2,1)}, bf16[192,256]{1,0:T(8,128)(2,1)S(1)}, u32[]{:S(2)}, u32[]{:S(2)}) collective-permute-start(bf16[192,256]{1,0:T(8,128)(2,1)} %get-tuple-element.81), channel_id=1, source_target_pairs={{0,1},{1,0},{2,3},{3,2},{4,5},{5,4},{6,7},{7,6},{8,9},{9,8},{10,11... | collective-permute-start | bytes 294920 | tf_op jit(solution)/shard_map/ppermute | solution.py:494
  45.3 30.3 %collective-permute-start.16 = (bf16[192,256]{1,0:T(8,128)(2,1)}, bf16[192,256]{1,0:T(8,128)(2,1)S(1)}, u32[]{:S(2)}, u32[]{:S(2)}) collective-permute-start(bf16[192,256]{1,0:T(8,128)(2,1)} %get-tuple-element.82), channel_id=1, source_target_pairs={{0,2},{1,3},{2,0},{3,1},{4,6},{5,7},{6,4},{7,5},{8,10},{9,11},{10,... | collective-permute-start | bytes 294920 | tf_op jit(solution)/shard_map/ppermute | solution.py:494
  47.1 28.7 %collective-permute-start.17 = (bf16[192,256]{1,0:T(8,128)(2,1)}, bf16[192,256]{1,0:T(8,128)(2,1)S(1)}, u32[]{:S(2)}, u32[]{:S(2)}) collective-permute-start(bf16[192,256]{1,0:T(8,128)(2,1)} %get-tuple-element.83), channel_id=1, source_target_pairs={{0,3},{1,2},{2,1},{3,0},{4,7},{5,6},{6,5},{7,4},{8,11},{9,10},{10,... | collective-permute-start | bytes 294920 | tf_op jit(solution)/shard_map/ppermute | solution.py:494
  54.7 22.4 %collective-permute-start.10 = (bf16[192,256]{1,0:T(8,128)(2,1)}, bf16[192,256]{1,0:T(8,128)(2,1)S(1)}, u32[]{:S(2)}, u32[]{:S(2)}) collective-permute-start(bf16[192,256]{1,0:T(8,128)(2,1)} %get-tuple-element.78), channel_id=1, source_target_pairs={{0,2},{1,3},{2,0},{3,1},{4,6},{5,7},{6,4},{7,5},{8,10},{9,11},{10,... | collective-permute-start | bytes 294920 | tf_op jit(solution)/shard_map/ppermute | solution.py:494
  56.3 21.8 %collective-permute-start.11 = (bf16[192,256]{1,0:T(8,128)(2,1)}, bf16[192,256]{1,0:T(8,128)(2,1)S(1)}, u32[]{:S(2)}, u32[]{:S(2)}) collective-permute-start(bf16[192,256]{1,0:T(8,128)(2,1)} %get-tuple-element.79), channel_id=1, source_target_pairs={{0,3},{1,2},{2,1},{3,0},{4,7},{5,6},{6,5},{7,4},{8,11},{9,10},{10,... | collective-permute-start | bytes 294920 | tf_op jit(solution)/shard_map/ppermute | solution.py:494
  127.2 125.8 %collective-permute-start.54 = (bf16[2,2,2,2,96,768]{5,4,0,3,2,1:T(8,128)(2,1)}, bf16[2,2,2,2,96,768]{5,4,0,3,2,1:T(8,128)(2,1)}, u32[]{:S(2)}, u32[]{:S(2)}) collective-permute-start(bf16[2,2,2,2,96,768]{5,4,0,3,2,1:T(8,128)(2,1)} %fusion), channel_id=1, source_target_pairs={{0,1},{1,0},{2,3},{3,2},{4,5},{5,4},{6,7},{7,6},{8,9},{9,8},{10,11... | collective-permute-start | bytes 7077896 | tf_op jit(solution)/shard_map/ppermute | solution.py:421
  131.8 125.1 %collective-permute-start.49 = (bf16[2,2,2,2,24,3072]{5,4,3,2,1,0:T(8,128)(2,1)}, bf16[2,2,2,2,24,3072]{5,4,3,2,1,0:T(8,128)(2,1)S(1)}, u32[]{:S(2)}, u32[]{:S(2)}) collective-permute-start(bf16[2,2,2,2,24,3072]{5,4,3,2,1,0:T(8,128)(2,1)} %fusion.1), channel_id=1, source_target_pairs={{0,1},{1,0},{2,3},{3,2},{4,5},{5,4},{6,7},{7,6},{8,9},{9,8},{10,11... | collective-permute-start | bytes 7077896 | tf_op jit(solution)/shard_map/ppermute | solution.py:421
  136.2 18.8 %collective-permute-start.23 = (bf16[192,256]{1,0:T(8,128)(2,1)S(1)}, bf16[192,256]{1,0:T(8,128)(2,1)S(1)}, u32[]{:S(2)}, u32[]{:S(2)}) collective-permute-start(bf16[192,256]{1,0:T(8,128)(2,1)S(1)} %copy-done.40), channel_id=1, source_target_pairs={{0,1},{1,0},{2,3},{3,2},{4,5},{5,4},{6,7},{7,6},{8,9},{9,8},{10,11... | collective-permute-start | bytes 294920 | tf_op jit(solution)/shard_map/ppermute | solution.py:494
  137.9 17.6 %collective-permute-start.24 = (bf16[192,256]{1,0:T(8,128)(2,1)S(1)}, bf16[192,256]{1,0:T(8,128)(2,1)S(1)}, u32[]{:S(2)}, u32[]{:S(2)}) collective-permute-start(bf16[192,256]{1,0:T(8,128)(2,1)S(1)} %copy-done.39), channel_id=1, source_target_pairs={{0,2},{1,3},{2,0},{3,1},{4,6},{5,7},{6,4},{7,5},{8,10},{9,11},{10,... | collective-permute-start | bytes 294920 | tf_op jit(solution)/shard_map/ppermute | solution.py:494
  139.1 17.7 %collective-permute-start.25 = (bf16[192,256]{1,0:T(8,128)(2,1)S(1)}, bf16[192,256]{1,0:T(8,128)(2,1)S(1)}, u32[]{:S(2)}, u32[]{:S(2)}) collective-permute-start(bf16[192,256]{1,0:T(8,128)(2,1)S(1)} %copy-done.37), channel_id=1, source_target_pairs={{0,3},{1,2},{2,1},{3,0},{4,7},{5,6},{6,5},{7,4},{8,11},{9,10},{10,... | collective-permute-start | bytes 294920 | tf_op jit(solution)/shard_map/ppermute | solution.py:494
  194.3 23.2 %collective-permute-start.41 = (f32[2,2,1,336]{3,2,1,0:T(1,128)S(1)}, f32[2,2,1,336]{3,2,1,0:T(1,128)S(1)}, u32[]{:S(2)}, u32[]{:S(2)}) collective-permute-start(f32[2,2,1,336]{3,2,1,0:T(1,128)S(1)} %fusion.33), channel_id=1, source_target_pairs={{0,8},{4,12},{8,0},{12,4},{16,24},{20,28},{24,16},{28,20},{1,9},{5... | collective-permute-start | bytes 16136 | tf_op jit(solution)/shard_map/ppermute | solution.py:421
  219.0 22.7 %collective-permute-start.44 = (bf16[2,2,2,2,24,768]{5,4,3,2,1,0:T(8,128)(2,1)S(1)}, bf16[2,2,2,2,24,768]{5,4,3,2,1,0:T(8,128)(2,1)S(1)}, u32[]{:S(2)}, u32[]{:S(2)}) collective-permute-start(bf16[2,2,2,2,24,768]{5,4,3,2,1,0:T(8,128)(2,1)S(1)} %fusion.6), channel_id=1, source_target_pairs={{0,1},{1,0},{2,3},{3,2},{4,5},{5,4},{6,7},{7,6},{8,9},{9,8},{10,11... | collective-permute-start | bytes 1769480 | tf_op jit(solution)/shard_map/ppermute | solution.py:421
  226.7 33.1 %collective-permute-start.31 = (bf16[2,256,768]{2,1,0:T(8,128)(2,1)}, bf16[2,256,768]{2,1,0:T(8,128)(2,1)S(1)}, u32[]{:S(2)}, u32[]{:S(2)}) collective-permute-start(bf16[2,256,768]{2,1,0:T(8,128)(2,1)} %get-tuple-element.119), channel_id=1, source_target_pairs={{0,1},{1,0},{2,3},{3,2},{4,5},{5,4},{6,7},{7,6},{8,9},{9,8},{10,11... | collective-permute-start | bytes 2359304 | tf_op jit(solution)/shard_map/ppermute | solution.py:494
  241.7 19.7 %collective-permute-start.26 = (bf16[2,256,768]{2,1,0:T(8,128)(2,1)}, bf16[2,256,768]{2,1,0:T(8,128)(2,1)S(1)}, u32[]{:S(2)}, u32[]{:S(2)}) collective-permute-start(bf16[2,256,768]{2,1,0:T(8,128)(2,1)} %get-tuple-element.107), channel_id=1, source_target_pairs={{0,1},{1,0},{2,3},{3,2},{4,5},{5,4},{6,7},{7,6},{8,9},{9,8},{10,11... | collective-permute-start | bytes 2359304 | tf_op jit(solution)/shard_map/ppermute | solution.py:494
  256.9 31.3 %collective-permute-start.55 = (bf16[2,2,2,96,768]{4,3,2,1,0:T(8,128)(2,1)S(1)}, bf16[2,2,2,96,768]{4,3,2,1,0:T(8,128)(2,1)S(1)}, u32[]{:S(2)}, u32[]{:S(2)}) collective-permute-start(bf16[2,2,2,96,768]{4,3,2,1,0:T(8,128)(2,1)S(1)} %copy.56), channel_id=1, source_target_pairs={{0,2},{1,3},{2,0},{3,1},{4,6},{5,7},{6,4},{7,5},{8,10},{9,11},{10,... | collective-permute-start | bytes 3538952 | tf_op jit(solution)/shard_map/ppermute | solution.py:421
  259.8 32.0 %collective-permute-start.50 = (bf16[2,2,2,24,3072]{4,3,2,1,0:T(8,128)(2,1)S(1)}, bf16[2,2,2,24,3072]{4,3,2,1,0:T(8,128)(2,1)S(1)}, u32[]{:S(2)}, u32[]{:S(2)}) collective-permute-start(bf16[2,2,2,24,3072]{4,3,2,1,0:T(8,128)(2,1)S(1)} %fusion.3), channel_id=1, source_target_pairs={{0,4},{4,0},{8,12},{12,8},{16,20},{20,16},{24,28},{28,24},{1,5},{5... | collective-permute-start | bytes 3538952 | tf_op jit(solution)/shard_map/ppermute | solution.py:421
  262.3 23.8 %collective-permute-start.37 = (bf16[24,576]{1,0:T(8,128)(2,1)S(1)}, bf16[24,576]{1,0:T(8,128)(2,1)S(1)}, u32[]{:S(2)}, u32[]{:S(2)}) collective-permute-start(bf16[24,576]{1,0:T(8,128)(2,1)S(1)} %get-tuple-element.145), channel_id=1, source_target_pairs={{0,2},{1,3},{2,0},{3,1},{4,6},{5,7},{6,4},{7,5},{8,10},{9,11},{10,... | collective-permute-start | bytes 82952 | tf_op jit(solution)/shard_map/ppermute | solution.py:494
  264.4 22.6 %collective-permute-start.38 = (bf16[24,576]{1,0:T(8,128)(2,1)S(1)}, bf16[24,576]{1,0:T(8,128)(2,1)S(1)}, u32[]{:S(2)}, u32[]{:S(2)}) collective-permute-start(bf16[24,576]{1,0:T(8,128)(2,1)S(1)} %get-tuple-element.144), channel_id=1, source_target_pairs={{0,3},{1,2},{2,1},{3,0},{4,7},{5,6},{6,5},{7,4},{8,11},{9,10},{10,... | collective-permute-start | bytes 82952 | tf_op jit(solution)/shard_map/ppermute | solution.py:494
  266.0 29.6 %collective-permute-start.46 = (bf16[2,2,24,768]{3,2,1,0:T(8,128)(2,1)S(1)}, bf16[2,2,24,768]{3,2,1,0:T(8,128)(2,1)S(1)}, u32[]{:S(2)}, u32[]{:S(2)}) collective-permute-start(bf16[2,2,24,768]{3,2,1,0:T(8,128)(2,1)S(1)} %fusion.16), channel_id=1, source_target_pairs={{0,8},{4,12},{8,0},{12,4},{16,24},{20,28},{24,16},{28,20},{1,9},{5... | collective-permute-start | bytes 442376 | tf_op jit(solution)/shard_map/ppermute | solution.py:421
  286.1 36.6 %collective-permute-start.32 = (bf16[1,256,768]{2,1,0:T(8,128)(2,1)}, bf16[1,256,768]{2,1,0:T(8,128)(2,1)}, u32[]{:S(2)}, u32[]{:S(2)}) collective-permute-start(bf16[1,256,768]{2,1,0:T(8,128)(2,1)} %add_convert_fusion), channel_id=1, source_target_pairs={{0,2},{1,3},{2,0},{3,1},{4,6},{5,7},{6,4},{7,5},{8,10},{9,11},{10,... | collective-permute-start | bytes 1179656 | tf_op jit(solution)/shard_map/ppermute | solution.py:494
  286.9 35.7 %collective-permute-start.27 = (bf16[1,256,768]{2,1,0:T(8,128)(2,1)}, bf16[1,256,768]{2,1,0:T(8,128)(2,1)}, u32[]{:S(2)}, u32[]{:S(2)}) collective-permute-start(bf16[1,256,768]{2,1,0:T(8,128)(2,1)} %add_convert_fusion.1), channel_id=1, source_target_pairs={{0,2},{1,3},{2,0},{3,1},{4,6},{5,7},{6,4},{7,5},{8,10},{9,11},{10,... | collective-permute-start | bytes 1179656 | tf_op jit(solution)/shard_map/ppermute | solution.py:494
  291.2 19.1 %collective-permute-start.56 = (bf16[2,2,96,768]{3,2,1,0:T(8,128)(2,1)}, bf16[2,2,96,768]{3,2,1,0:T(8,128)(2,1)}, u32[]{:S(2)}, u32[]{:S(2)}) collective-permute-start(bf16[2,2,96,768]{3,2,1,0:T(8,128)(2,1)} %copy.59), channel_id=1, source_target_pairs={{0,4},{4,0},{8,12},{12,8},{16,20},{20,16},{24,28},{28,24},{1,5},{5... | collective-permute-start | bytes 1769480 | tf_op jit(solution)/shard_map/ppermute | solution.py:421
  294.1 19.3 %collective-permute-start.51 = (bf16[2,2,24,3072]{3,2,1,0:T(8,128)(2,1)}, bf16[2,2,24,3072]{3,2,1,0:T(8,128)(2,1)}, u32[]{:S(2)}, u32[]{:S(2)}) collective-permute-start(bf16[2,2,24,3072]{3,2,1,0:T(8,128)(2,1)} %fusion.5), channel_id=1, source_target_pairs={{0,8},{4,12},{8,0},{12,4},{16,24},{20,28},{24,16},{28,20},{1,9},{5... | collective-permute-start | bytes 1769480 | tf_op jit(solution)/shard_map/ppermute | solution.py:421
  319.5 18.1 %collective-permute-start.52 = (bf16[2,24,3072]{2,1,0:T(8,128)(2,1)}, bf16[2,24,3072]{2,1,0:T(8,128)(2,1)}, u32[]{:S(2)}, u32[]{:S(2)}) collective-permute-start(bf16[2,24,3072]{2,1,0:T(8,128)(2,1)} %fusion.8), channel_id=1, source_target_pairs={{0,16},{4,20},{8,24},{12,28},{16,0},{20,4},{24,8},{28,12},{1,17},{... | collective-permute-start | bytes 884744 | tf_op jit(solution)/shard_map/ppermute | solution.py:421
  (87 other events, 1017.4 us)

commit v2 on v1

--- a/solution.py
+++ b/solution.py
@@ -233,60 +233,160 @@
     )(info, *gats, n1, qkv, full, lse, w, dw_in, sums_in)
 
 
-def middle_kernel(blocks, images, steps, info, *refs):
+def flip(index, k):
+    return index + (1 << k) * (1 - 2 * lax.rem(lax.div(index, 1 << k), 2))
+
+
+def flip_all(index, mask):
+    for k in range(mask.bit_length()):
+        if mask >> k & 1:
+            index = flip(index, k)
+    return index
+
+
+def meet(peers):
+    barrier = pltpu.get_barrier_semaphore()
+    for peer in peers:
+        pl.semaphore_signal(barrier, inc=1, device_id=peer, device_id_type=pl.DeviceIdType.MESH)
+    pl.semaphore_wait(barrier, len(peers))
+
+
+def middle_kernel(blocks, images, steps, bits, *refs):
     count = blocks * images
     atts = refs[:count]
     x, cot, vec, ow, b1, w1, w2 = refs[count : count + 7]
-    out, gmid, dwo, dw1, dw2, gb1, sums = refs[count + 7 : count + 14]
-    gats = refs[count + 14 : 2 * count + 14]
-    middle, branch, n2, n2t, gm, mlp, gn2 = refs[2 * count + 14 :]
-    j = pl.program_id(0)
-    me = info[1]
+    out, gmid, g1, g2, gb1, sums = refs[count + 7 : count + 13]
+    gats = refs[count + 13 : 2 * count + 13]
+    (middle, branch, n2, gm, gn2, act, gpre, keep1, keep2, s1, r1, s2, r2, ds1, dr1, ds2, dr2, *second) = refs[
+        2 * count + 13 :
+    ]
+    t = pl.program_id(0)
+    me, im = lax.axis_index("blk"), lax.axis_index("img")
+    core = lax.rem(me, 2)
     hw, rows = atts[0].shape
-    gain2, shift2, s1, s2 = vec[2:3, :], vec[3:4, :], vec[4:5, :], vec[5:6, :]
+    d = x.shape[1]
+    width = d // 2
+    gain2, shift2, sc1, sc2 = vec[2:3, :], vec[3:4, :], vec[4:5, :], vec[5:6, :]
     bias_o, bias2 = vec[6:7, :], vec[7:8, :]
-
-    @pl.when(j == 0)
+    mine = pl.ds(pl.multiple_of(core * width, width), width)
+    other = pl.ds(pl.multiple_of((1 - core) * width, width), width)
+    mesh_id = pl.DeviceIdType.MESH
+    near = {"blk": flip(me, 0)}
+    if bits:
+        half1, half2, u1, v1, u2, v2, us1, ur1, us2, ur2 = second
+        peers = [{"img": flip(im, k)} for k in bits]
+        where = [lax.rem(lax.div(im, 1 << k), 2) for k in bits]
+
+    def cross(src, dst, send, recv, k, peer):
+        return pltpu.make_async_remote_copy(
+            src_ref=src.at[k],
+            dst_ref=dst.at[k],
+            send_sem=send.at[k],
+            recv_sem=recv.at[k],
+            device_id=peer,
+            device_id_type=mesh_id,
+        )
+
+    def split(keep, got, half, send, k, bit):
+        parts, low = half.shape[0], half.shape[1]
+        for i in range(parts):
+            to = pl.ds(pl.multiple_of((2 * i + 1 - bit) * low, low), low)
+            on = pl.ds(pl.multiple_of((2 * i + bit) * low, low), low)
+            send[k, i] = (keep[to, :] + got[k, to, :].astype(f32)).astype(bf16)
+            half[i] = keep[on, :] + got[k, on, :].astype(f32)
+
+    def after_core(k, only_first):
+        cross(s1, r1, ds1, dr1, k, near).wait()
+        if bits:
+            split(keep1, r1, half1, u1, k, where[0])
+            cross(u1, v1, us1, ur1, k, peers[0]).start()
+        else:
+            g1[:, pl.ds(pl.multiple_of(k * width, width), width)] = (keep1[...] + r1[k].astype(f32)).astype(bf16)
+        if only_first:
+            return
+        cross(s2, r2, ds2, dr2, k, near).wait()
+        if bits:
+            split(keep2, r2, half2, u2, k, where[1])
+            cross(u2, v2, us2, ur2, k, peers[1]).start()
+        else:
+            g2[k] = (keep2[...] + r2[k].astype(f32)).astype(bf16)
+
+    def after_bit(k, only_first):
+        if not bits:
+            return
+        cross(u1, v1, us1, ur1, k, peers[0]).wait()
+        columns = pl.ds(pl.multiple_of(k * width, width), width)
+        for i in range(half1.shape[0]):
+            g1[i, :, columns] = (half1[i] + v1[k, i].astype(f32)).astype(bf16)
+        if only_first:
+            return
+        cross(u2, v2, us2, ur2, k, peers[1]).wait()
+        for i in range(half2.shape[0]):
+            g2[k, i] = (half2[i] + v2[k, i].astype(f32)).astype(bf16)
+
+    @pl.when(t == 0)
     def _():
+        meet([near] + (peers if bits else []))
         for i in range(images):
             rs = slice(i * rows, (i + 1) * rows)
-            total = jnp.zeros((rows, x.shape[1]), f32)
+            total = jnp.zeros((rows, d), f32)
             for m in range(blocks):
-                start = pl.multiple_of((me ^ m) * hw, hw)
-                total += dot_nn(atts[i * blocks + m][...].T, ow[pl.ds(start, hw), :])
+                start = pl.multiple_of(flip_all(me, m) * hw, hw)
+                total += dot_tn(atts[i * blocks + m][...], ow[pl.ds(start, hw), :])
             total = total + bias_o
             branch[rs, :] = total
-            mid = x[rs, :].astype(f32) + s1 * total
+            mid = x[rs, :].astype(f32) + sc1 * total
             middle[rs, :] = mid
             z, _ = standardize(mid)
-            low = (z * gain2 + shift2).astype(bf16)
-            n2[rs, :] = low
-            n2t[:, rs] = low.T
-            gm[rs, :] = (s2 * cot[rs, :].astype(f32)).astype(bf16)
-        mlp[...] = jnp.zeros_like(mlp)
+            n2[rs, :] = (z * gain2 + shift2).astype(bf16)
+            gm[rs, :] = (sc2 * cot[rs, :].astype(f32)).astype(bf16)
+        gmid[...] = jnp.zeros_like(gmid)
         gn2[...] = jnp.zeros_like(gn2)
 
-    hp = dot_nn(n2[...], w1[...]) + b1[...]
-    phi = 0.5 + 0.5 * lax.erf(hp * inv_sqrt2)
-    act = (hp * phi).astype(bf16)
-    slope = phi + hp * (jnp.exp(-0.5 * hp * hp) * inv_sqrt2pi)
-    mlp[...] += dot_nn(act, w2[...])
-    gpre_full = dot_nt(gm[...], w2[...]) * slope
-    gpre = gpre_full.astype(bf16)
-    dw2[...] = dot_tn(act, gm[...])
-    dw1[...] = dot_nn(n2t[...], gpre)
-    gb1[...] = jnp.sum(gpre.astype(f32), axis=0, keepdims=True)
-    gn2[...] += dot_nt(gpre, w1[...])
-
-    @pl.when(j == steps - 1)
+    @pl.when(t < steps)
     def _():
-        zero = jnp.zeros((1, x.shape[1]), f32)
+        bias_sum = jnp.zeros((1, w1.shape[1]), f32)
+        for i in range(images):
+            rs = slice(i * rows, (i + 1) * rows)
+            hp = dot_nn(n2[rs, :], w1[...]) + b1[...]
+            phi = 0.5 + 0.5 * lax.erf(hp * inv_sqrt2)
+            act[rs, :] = (hp * phi).astype(bf16)
+            slope = phi + hp * (jnp.exp(-0.5 * hp * hp) * inv_sqrt2pi)
+            low = (dot_nt(gm[rs, :], w2[...]) * slope).astype(bf16)
+            gpre[rs, :] = low
+            bias_sum += jnp.sum(low.astype(f32), axis=0, keepdims=True)
+        gb1[...] = bias_sum
+
+    @pl.when(jnp.logical_and(t >= 2, t < steps))
+    def _():
+        after_bit(t - 2, False)
+
+    @pl.when(jnp.logical_and(t >= 1, t < steps))
+    def _():
+        after_core(t - 1, False)
+
+    @pl.when(t < steps)
+    def _():
+        s1[t] = dot_tn(n2[...], gpre[:, other]).astype(bf16)
+        cross(s1, r1, ds1, dr1, t, near).start()
+        s2[t] = dot_tn(act[...], gm[:, other]).astype(bf16)
+        cross(s2, r2, ds2, dr2, t, near).start()
+        keep1[...] = dot_tn(n2[...], gpre[:, mine])
+        keep2[...] = dot_tn(act[...], gm[:, mine])
+        gmid[...] += dot_nn(act[...], w2[...])
+        gn2[...] += dot_nt(gpre[...], w1[...])
+
+    @pl.when(t == steps)
+    def _():
+        after_bit(steps - 2, False)
+        after_core(steps - 1, False)
+        zero = jnp.zeros((1, d), f32)
         g_s2, g_b2, g_gain, g_shift, g_s1, g_bo = zero, zero, zero, zero, zero, zero
         for i in range(images):
             rs = slice(i * rows, (i + 1) * rows)
             mid = middle[rs, :]
-            mo = mlp[rs, :] + bias2
-            out[rs, :] = (mid + s2 * mo).astype(bf16)
+            mo = gmid[rs, :] + bias2
+            out[rs, :] = (mid + sc2 * mo).astype(bf16)
             go = cot[rs, :].astype(f32)
             g_s2 += jnp.sum(go * mo, axis=0, keepdims=True)
             g_b2 += jnp.sum(gm[rs, :].astype(f32), axis=0, keepdims=True)
@@ -300,58 +400,88 @@
             )
             gmid[rs, :] = gmd
             g_s1 += jnp.sum(gmd * branch[rs, :], axis=0, keepdims=True)
-            gb = (s1 * gmd).astype(bf16)
+            gb = (sc1 * gmd).astype(bf16)
             n2[rs, :] = gb
             g_bo += jnp.sum(gb.astype(f32), axis=0, keepdims=True)
+        sums[...] = jnp.concatenate([g_s2, g_b2, g_gain, g_shift, g_s1, g_bo, zero, zero], axis=0)
+        for columns, sent in ((other, True), (mine, False)):
+            for m in range(blocks):
+                start = pl.ds(pl.multiple_of(flip_all(me, m) * hw, hw), hw)
+                term = jnp.zeros((hw, width), f32)
+                for i in range(images):
+                    term += dot_nn(atts[i * blocks + m][...], n2[i * rows : (i + 1) * rows, columns])
+                if sent:
+                    s1[steps, start, :] = term.astype(bf16)
+                else:
+                    keep1[start, :] = term
+            if sent:
+                cross(s1, r1, ds1, dr1, steps, near).start()
         for m in range(blocks):
-            start = pl.multiple_of((me ^ m) * hw, hw)
-            term = jnp.zeros((hw, x.shape[1]), f32)
+            start = pl.ds(pl.multiple_of(flip_all(me, m) * hw, hw), hw)
             for i in range(images):
-                gb = n2[i * rows : (i + 1) * rows, :]
-                term += dot_nn(atts[i * blocks + m][...], gb)
-                gats[i * blocks + m][...] = dot_nt(ow[pl.ds(start, hw), :], gb).astype(bf16)
-            dwo[pl.ds(start, hw), :] = term
-        sums[...] = jnp.concatenate([g_s2, g_b2, g_gain, g_shift, g_s1, g_bo, zero, zero], axis=0)
-
-
-def middle_layers(info, atts, x, cot, vec, ow, b1, w1, w2, blocks, images):
+                gats[i * blocks + m][...] = dot_nt(ow[start, :], n2[i * rows : (i + 1) * rows, :]).astype(bf16)
+        after_bit(steps - 1, False)
+        after_core(steps, True)
+        after_bit(steps, True)
+
+
+def middle_layers(atts, x, cot, vec, ow, b1, w1, w2, blocks, images, share, bits):
     hw, rows = atts[0].shape
     total, d = x.shape
     ff = w1.shape[1]
-    chunk = 512
+    chunk, width = d, d // 2
     steps = ff // chunk
-    whole = lambda shape: pl.BlockSpec(shape, lambda j: (0,) * len(shape))
+    once = dict(pipeline_mode=pl.Buffered(1))
+    whole = lambda shape: pl.BlockSpec(shape, lambda j: (0,) * len(shape), **once)
+    last = lambda j: jnp.minimum(j, steps - 1)
+    if bits:
+        low1, low2 = (blocks * share) << bits[0], (blocks * ff * share // d) << bits[1]
+        shape1 = (d // (2 * low1), low1)
+        shape2 = (chunk // (2 * low2), low2)
+        g1_shape = shape1 + ((steps + 1) * width,)
+        g2_shape = (steps,) + shape2 + (width,)
+        second = [
+            pltpu.VMEM(shape1 + (width,), f32),
+            pltpu.VMEM(shape2 + (width,), f32),
+            pltpu.VMEM((steps + 1,) + shape1 + (width,), bf16),
+            pltpu.VMEM((steps + 1,) + shape1 + (width,), bf16),
+            pltpu.VMEM((steps,) + shape2 + (width,), bf16),
+            pltpu.VMEM((steps,) + shape2 + (width,), bf16),
+            pltpu.SemaphoreType.DMA((steps + 1,)),
+            pltpu.SemaphoreType.DMA((steps + 1,)),
+            pltpu.SemaphoreType.DMA((steps,)),
+            pltpu.SemaphoreType.DMA((steps,)),
+        ]
+    else:
+        g1_shape, g2_shape, second = (d, (steps + 1) * width), (steps, chunk, width), []
     return pl.pallas_call(
-        partial(middle_kernel, blocks, images, steps),
+        partial(middle_kernel, blocks, images, steps, bits),
         name="middle_layers",
-        grid=(steps,),
-        in_specs=[pl.BlockSpec(memory_space=pltpu.SMEM)]
-        + [whole((hw, rows))] * (blocks * images)
+        grid=(steps + 1,),
+        in_specs=[whole((hw, rows))] * (blocks * images)
         + [
             whole((total, d)),
             whole((total, d)),
             whole(vec.shape),
             whole(ow.shape),
-            pl.BlockSpec((1, chunk), lambda j: (0, j)),
-            pl.BlockSpec((d, chunk), lambda j: (0, j)),
-            pl.BlockSpec((chunk, d), lambda j: (j, 0)),
+            pl.BlockSpec((1, chunk), lambda j: (0, last(j))),
+            pl.BlockSpec((d, chunk), lambda j: (0, last(j))),
+            pl.BlockSpec((chunk, d), lambda j: (last(j), 0)),
         ],
         out_specs=[
             whole((total, d)),
             whole((total, d)),
-            whole((d, d)),
-            pl.BlockSpec((d, chunk), lambda j: (0, j)),
-            pl.BlockSpec((chunk, d), lambda j: (j, 0)),
-            pl.BlockSpec((1, chunk), lambda j: (0, j)),
+            whole(g1_shape),
+            whole(g2_shape),
+            pl.BlockSpec((1, chunk), lambda j: (0, last(j))),
             whole((8, d)),
         ]
         + [whole((hw, rows))] * (blocks * images),
         out_shape=[
             jax.ShapeDtypeStruct((total, d), bf16),
             jax.ShapeDtypeStruct((total, d), f32),
-            jax.ShapeDtypeStruct((d, d), f32),
-            jax.ShapeDtypeStruct((d, ff), f32),
-            jax.ShapeDtypeStruct((ff, d), f32),
+            jax.ShapeDtypeStruct(g1_shape, bf16),
+            jax.ShapeDtypeStruct(g2_shape, bf16),
             jax.ShapeDtypeStruct((1, ff), f32),
             jax.ShapeDtypeStruct((8, d), f32),
         ]
@@ -360,16 +490,27 @@
             pltpu.VMEM((total, d), f32),
             pltpu.VMEM((total, d), f32),
             pltpu.VMEM((total, d), bf16),
-            pltpu.VMEM((d, total), bf16),
             pltpu.VMEM((total, d), bf16),
             pltpu.VMEM((total, d), f32),
-            pltpu.VMEM((total, d), f32),
-        ],
-        compiler_params=params(dimension_semantics=("arbitrary",)),
+            pltpu.VMEM((total, chunk), bf16),
+            pltpu.VMEM((total, chunk), bf16),
+            pltpu.VMEM((d, width), f32),
+            pltpu.VMEM((chunk, width), f32),
+            pltpu.VMEM((steps + 1, d, width), bf16),
+            pltpu.VMEM((steps + 1, d, width), bf16),
+            pltpu.VMEM((steps, chunk, width), bf16),
+            pltpu.VMEM((steps, chunk, width), bf16),
+            pltpu.SemaphoreType.DMA((steps + 1,)),
+            pltpu.SemaphoreType.DMA((steps + 1,)),
+            pltpu.SemaphoreType.DMA((steps,)),
+            pltpu.SemaphoreType.DMA((steps,)),
+        ]
+        + second,
+        compiler_params=params(dimension_semantics=("arbitrary",), collective_id=1, has_side_effects=True),
         cost_estimate=pl.CostEstimate(
-            flops=12 * total * d * ff + 6 * total * d * d, bytes_accessed=40_000_000, transcendentals=0
+            flops=12 * total * d * ff + 6 * total * d * d, bytes_accessed=30_000_000, transcendentals=0
         ),
-    )(info, *atts, x, cot, vec, ow, b1, w1, w2)
+    )(*atts, x, cot, vec, ow, b1, w1, w2)
 
 
 def finish_kernel(x, gmid, gain, *refs):
@@ -502,8 +643,13 @@
             n1, qkv, full, lse, *outs = forward_image(infos[i], xs, vec, w, wb, nh)
             saved.append((n1, qkv, full, lse))
             atts.extend([outs[0]] + [swap_blk(outs[m], m) for m in range(1, blocks)])
-        out, gmid, dwo, dw1, dw2, gb1, sums, *gats = middle_layers(
-            infos[0],
+        n = places.n_img * blocks
+        share = d // n
+        ff = fc1_weight.shape[1]
+        half = d // 2
+        y_bit, z_bit = 0, 1
+        bits = (z_bit, y_bit) if share % 8 == 0 and places.img_bits > 1 else ()
+        out, gmid, g1, g2, gb1, sums, *gats = middle_layers(
             atts,
             tokens.reshape(total, d),
             cotangent.reshape(total, d),
@@ -514,17 +660,27 @@
             fc2_weight,
             blocks,
             images,
+            share,
+            bits,
         )
-        n = places.n_img * blocks
-        share = d // n
-        ff = fc1_weight.shape[1]
-        z_dims = [("img", k) for k in range(places.img_bits)]
-        core, far_x = ("blk", 0), ("blk", 1)
-        order_y = [core] + z_dims + [far_x]
-        order_x = [core, far_x] + z_dims
-        grad_fc2 = scatter_sum(places, dw2.reshape(n, ff // n, d), places.dims, order_x)
-        grad_fc1 = scatter_sum(places, dw1.reshape(n, share, ff), places.dims, order_y)
-        grad_out = scatter_sum(places, dwo.reshape(n, share, d), places.dims, order_y)
+        chips = [dim for dim in places.dims if dim != ("blk", 0)]
+        left1 = [dim for dim in chips if not bits or dim != ("img", bits[0])]
+        left2 = [dim for dim in chips if not bits or dim != ("img", bits[1])]
+        g1 = scatter_sum(places, g1.reshape(2 ** len(left1), 2 * share, -1), left1, left1[::-1])
+        g2 = scatter_sum(places, g2.reshape(2 ** len(left2), 2 * (ff // n), half), left2, left2[::-1])
+
+        def both_cores(value):
+            value = value.reshape((2, -1) + value.shape[1:])
+            core = places.bit(("blk", 0))
+            own = lax.dynamic_index_in_dim(value, core, 0, keepdims=False)
+            far = swap_blk(lax.dynamic_index_in_dim(value, 1 - core, 0, keepdims=False).astype(bf16), 1).astype(f32)
+            return jnp.where(core == 0, own, far), jnp.where(core == 0, far, own)
+
+        first, second = both_cores(g1)
+        merged = jnp.concatenate([first.reshape(share, -1, half), second.reshape(share, -1, half)], axis=2)
+        grad_fc1 = merged[:, : ff // d].reshape(share, ff)
+        grad_out = merged[:, ff // d]
+        grad_fc2 = jnp.concatenate(both_cores(g2), axis=1)
 
         dw = jnp.zeros((d, 3 * hw), f32)
         sums1 = jnp.zeros((8, d), f32)
@@ -538,7 +694,7 @@
         grad_tokens = finish(tokens, gmid, vec[0:1, :], terms)
 
         img_dims = [("img", k) for k in reversed(range(places.img_bits))]
-        part = scatter_sum(places, dw.reshape(places.n_img, blocks * share, 3 * hw), img_dims, z_dims)
+        part = scatter_sum(places, dw.reshape(places.n_img, blocks * share, 3 * hw), img_dims, img_dims[::-1])
         part = part.reshape(blocks, share, 3 * hw)
         pieces = [
             lax.dynamic_slice(part, (me ^ m, 0, 0), (1, share, 3 * hw))[0].astype(bf16) for m in range(blocks)
@@ -557,7 +713,7 @@
         small = jnp.stack([g_qb, g_vb, g_bo, g_n1g, g_n1b, g_n2g, g_n2b, g_b2, g_s1, g_s2])
         small = small.reshape(10, n, share).transpose(1, 0, 2).reshape(n, 1, 10 * share)
         small = jnp.concatenate([small, gb1.reshape(n, 1, ff // n)], axis=2)
-        small = scatter_sum(places, small, places.dims, order_y, link=f32)[0]
+        small = scatter_sum(places, small, places.dims, places.dims[::-1], link=f32)[0]
         v = [small[k * share : (k + 1) * share] for k in range(10)]
         g_b1 = small[10 * share :]
         return (

time: 347 us -> 300 us (0.86)
  starting transfers between devices: 75.8 us -> 42.8 us
  Pallas kernels: 126 us -> 153 us
  other arithmetic: 38.8 us -> 19.6 us
  waiting for transfers between devices: 73.3 us -> 60 us
  local copies, waits for them, and re-layouts: 29.9 us -> 20.2 us
    ppermute x23 -> x14, starting transfers between devices: 52.6 us -> 18.9 us  [swap(): return lax.ppermute(value, axis, [(i, i ^ 1 << k) for i in range(n)])]
    pallas_call x1, Pallas kernels: 39.8 us -> 61.8 us  [middle_layers(): pl.pallas_call(partial(middle_kernel, blocks, images, steps, bits), name=...]
    ppermute x36 -> x38, waiting for transfers between devices: 38.3 us -> 22.5 us  [swap_blk(): return lax.ppermute(value, 'blk', [(b, b ^ m) for b in range(blocks)])]
    convert_element_type x14 -> x6, other arithmetic: 20 us -> 4.34 us  [scatter_sum(): send = add({**known, dim: 1 - bit}).astype(link)]
    convert_element_type x6 -> x1, local copies, waits for them, and re-layouts: 11.9 us -> 0.05 us  [scatter_sum(): send = add({**known, dim: 1 - bit}).astype(link)]
    pallas_call x3, Pallas kernels: 39.5 us -> 43.6 us  [forward_image(): pl.pallas_call(partial(forward_kernel, blocks, nh, rows), name='attend_fo...]
    ppermute x23 -> x14, waiting for transfers between devices: 35 us -> 37.5 us  [swap(): return lax.ppermute(value, axis, [(i, i ^ 1 << k) for i in range(n)])]
    ppermute x36 -> x38, starting transfers between devices: 23.3 us -> 23.9 us  [swap_blk(): return lax.ppermute(value, 'blk', [(b, b ^ m) for b in range(blocks)])]
  transfers between devices with their start and end apart: 59 -> 52, of which waited for: 18 -> 17; matrix products, arithmetic and copies ran while one was open for 17% -> 10% of each run, Pallas kernels for 25% -> 26%
where the time goes in v2:
time: 300 us; the launch traced here: 297 us
  Pallas kernels  153 us (51%)
  waiting for transfers between devices  60 us (20%)
  starting transfers between devices  42.8 us (14%)
  local copies, waits for them, and re-layouts  20.2 us (7%)
  other arithmetic  19.6 us (7%)
    pallas_call x1, Pallas kernels, middle_layers(): pl.pallas_call(partial(middle_kernel, blocks, images, steps, bits), name=...  61.8 us
    pallas_call x3, Pallas kernels, forward_image(): pl.pallas_call(partial(forward_kernel, blocks, nh, rows), name='attend_fo...  43.6 us
    pallas_call x3, Pallas kernels, backward_image(): pl.pallas_call(partial(backward_kernel, blocks, nh, rows), name='attend_b...  41.2 us
    ppermute x14, waiting for transfers between devices, swap(): return lax.ppermute(value, axis, [(i, i ^ 1 << k) for i in range(n)])  37.5 us
    ppermute x38, starting transfers between devices, swap_blk(): return lax.ppermute(value, 'blk', [(b, b ^ m) for b in range(blocks)])  23.9 us
    ppermute x38, waiting for transfers between devices, swap_blk(): return lax.ppermute(value, 'blk', [(b, b ^ m) for b in range(blocks)])  22.5 us
    ppermute x14, starting transfers between devices, swap(): return lax.ppermute(value, axis, [(i, i ^ 1 << k) for i in range(n)])  18.9 us
  transfers between devices with their start and end apart: 52, of which 17 were waited for; matrix products, arithmetic and copies ran while one was open for 10% of the time, Pallas kernels for 26%

profile of v2, /device:TPU:0, one launch (start us, length us, event | category | flops | bytes accessed | tf_op | source)
XLA Modules:
  0.0 297.1 jit_solution(15352202880866765893)
XLA Ops:
  2.1 3.0 %collective-permute-start.13 = (bf16[256,768]{1,0:T(8,128)(2,1)S(1)}, bf16[256,768]{1,0:T(8,128)(2,1)}, u32[]{:S(2)}, u32[]{:S(2)}) collective-permute-start(bf16[256,768]{1,0:T(8,128)(2,1)S(1)} %get-tuple-element.134.refs_0_), channel_id=1, source_target_pairs={{0,2},{1,3},{2,0},{3,1},{4,6},{5,7},{6,4},{7,5},{8,10},{9,11},{10,... | collective-permute-start | bytes 1179656 | tf_op jit(solution)/shard_map/ppermute | solution.py:635
  5.6 1.7 collective-permute-start.1
  11.4 3.8 %collective-permute-done.13.refs_2_ = bf16[256,768]{1,0:T(8,128)(2,1)} collective-permute-done((bf16[256,768]{1,0:T(8,128)(2,1)S(1)}, bf16[256,768]{1,0:T(8,128)(2,1)}, u32[]{:S(2)}, u32[]{:S(2)}) %collective-permute-start.13) | collective-permute-done | bytes 393248 | tf_op jit(solution)/shard_map/ppermute | solution.py:635
  16.4 2.0 constant_dynamic-slice_fusion.18
  18.4 5.1 %collective-permute-done.7.refs_2_ = bf16[256,768]{1,0:T(8,128)(2,1)S(1)} collective-permute-done((bf16[256,768]{1,0:T(8,128)(2,1)S(1)}, bf16[256,768]{1,0:T(8,128)(2,1)S(1)}, u32[]{:S(2)}, u32[]{:S(2)}) %collective-permute-start.7) | collective-permute-done | bytes 393248 | tf_op jit(solution)/shard_map/ppermute | solution.py:635
  27.4 3.6 %collective-permute-done.1.refs_2_ = bf16[256,768]{1,0:T(8,128)(2,1)S(1)} collective-permute-done((bf16[256,768]{1,0:T(8,128)(2,1)S(1)}, bf16[256,768]{1,0:T(8,128)(2,1)S(1)}, u32[]{:S(2)}, u32[]{:S(2)}) %collective-permute-start.1) | collective-permute-done | bytes 393248 | tf_op jit(solution)/shard_map/ppermute | solution.py:635
  31.1 22.6 %attend_forward.5 = (bf16[4,256,768]{2,1,0:T(8,128)(2,1)}, bf16[4,256,576]{2,1,0:T(8,128)(2,1)}, f32[192,1024]{1,0:T(8,128)}, f32[8,1024]{1,0:T(8,128)}, bf16[19...) custom-call(s32[2]{0:T(128)} %pad_add_fusion.2.info, ...), custom_call_target="tpu_custom_call" | custom-call | flops 2516582400 | bytes 8000000 | tf_op jit(solution)/shard_map/attend_forward/pallas_call | solution.py:101
  54.2 1.7 collective-permute-start.16
  55.9 13.4 %attend_forward.4 = (bf16[4,256,768]{2,1,0:T(8,128)(2,1)}, bf16[4,256,576]{2,1,0:T(8,128)(2,1)}, f32[192,1024]{1,0:T(8,128)}, f32[8,1024]{1,0:T(8,128)}, bf16[19...) custom-call(s32[2]{0:T(128)} %pad_add_fusion.1.info, ...), custom_call_target="tpu_custom_call" | custom-call | flops 2516582400 | bytes 8000000 | tf_op jit(solution)/shard_map/attend_forward/pallas_call | solution.py:101
  69.3 1.6 collective-permute-start.10
  71.6 7.6 %attend_forward.3 = (bf16[4,256,768]{2,1,0:T(8,128)(2,1)}, bf16[4,256,576]{2,1,0:T(8,128)(2,1)}, f32[192,1024]{1,0:T(8,128)}, f32[8,1024]{1,0:T(8,128)}, bf16[19...) custom-call(s32[2]{0:T(128)} %pad_add_fusion.info, ...), custom_call_target="tpu_custom_call" | custom-call | flops 2516582400 | bytes 8000000 | tf_op jit(solution)/shard_map/attend_forward/pallas_call | solution.py:101
  82.2 3.5 %collective-permute-done.4.refs_2_ = bf16[192,256]{1,0:T(8,128)(2,1)S(1)} collective-permute-done((bf16[192,256]{1,0:T(8,128)(2,1)}, bf16[192,256]{1,0:T(8,128)(2,1)S(1)}, u32[]{:S(2)}, u32[]{:S(2)}) %collective-permute-start.4) | collective-permute-done | bytes 98336 | tf_op jit(solution)/shard_map/ppermute | solution.py:635
  87.3 61.8 %middle_layers.1 = (bf16[768,768]{1,0:T(8,128)(2,1)}, f32[768,768]{1,0:T(8,128)}, bf16[2,192,1920]{2,1,0:T(8,128)(2,1)}, bf16[4,1,384,384]{3,2,1,0:T(8,128)(2,1)...) custom-call(bf16[192,256]{1,0:T(8,128)(2,1)} %get-tuple-element.71.r, ...), custom_call_target="tpu_custom_call" | custom-call | flops 24461180928 | bytes 30000000 | tf_op jit(solution)/shard_map/middle_layers/pallas_call | solution.py:457
  149.2 1.4 collective-permute-start.19
  161.2 10.8 %attend_backward.3 = (f32[768,576]{1,0:T(8,128)}, f32[8,768]{1,0:T(8,128)}, bf16[2,256,768]{2,1,0:T(8,128)(2,1)}, bf16[2,256,768]{2,1,0:T(8,128)(2,1)}) custom-call(s32[2]{0:T(128)} %pad_add_fusion.info, bf16[192,256]{1,0:T(8,128)(2,1)} %get-tuple-element.85.refs_0_, bf16[192,256]{1,0:T(8,128)(2,1)} %copy-done.48, bf16[192,256]{1,0:T(8,128)(2,1)} %copy-done.51, ...), custom_call_target="tpu_custom_call" | custom-call | flops 5838471168 | bytes 12000000 | tf_op jit(solution)/shard_map/attend_backward/pallas_call | solution.py:206
  172.8 17.5 %attend_backward.4 = (f32[768,576]{1,0:T(8,128)}, f32[8,768]{1,0:T(8,128)}, bf16[2,256,768]{2,1,0:T(8,128)(2,1)}, bf16[2,256,768]{2,1,0:T(8,128)(2,1)}) custom-call(s32[2]{0:T(128)} %pad_add_fusion.1.info, bf16[192,256]{1,0:T(8,128)(2,1)} %get-tuple-element.95.refs_0_, bf16[192,256]{1,0:T(8,128)(2,1)} %copy-done.43, bf16[192,256]{1,0:T(8,128)(2,1)} %copy-done.44, ...), custom_call_target="tpu_custom_call" | custom-call | flops 5838471168 | bytes 12000000 | tf_op jit(solution)/shard_map/attend_backward/pallas_call | solution.py:206
  191.0 13.0 %attend_backward.5 = (f32[768,576]{1,0:T(8,128)}, f32[8,768]{1,0:T(8,128)}, bf16[2,256,768]{2,1,0:T(8,128)(2,1)}, bf16[2,256,768]{2,1,0:T(8,128)(2,1)}) custom-call(s32[2]{0:T(128)} %pad_add_fusion.2.info, bf16[192,256]{1,0:T(8,128)(2,1)} %get-tuple-element.107.refs_0_, bf16[192,256]{1,0:T(8,128)(2,1)} %copy-done.46, bf16[192,256]{1,0:T(8,128)(2,1)} %copy-done.49, ...), custom_call_target="tpu_custom_call" | custom-call | flops 5838471168 | bytes 12000000 | tf_op jit(solution)/shard_map/attend_backward/pallas_call | solution.py:206
  210.7 1.8 collective-permute-done.40
  214.2 2.1 collective-permute-done.41
  216.4 2.2 collective-permute-start.42
  220.3 3.5 %collective-permute-start.43 = (f32[1,336]{1,0:T(1,128)S(1)}, f32[1,336]{1,0:T(1,128)S(1)}, u32[]{:S(2)}, u32[]{:S(2)}) collective-permute-start(f32[1,336]{1,0:T(1,128)S(1)} %fusion.53), channel_id=1, source_target_pairs={{0,16},{4,20},{8,24},{12,28},{16,0},{20,4},{24,8},{28,12},{1,17},{... | collective-permute-start | bytes 4040 | tf_op jit(solution)/shard_map/ppermute | solution.py:562
  226.0 7.9 %collective-permute-done.33 = bf16[2,2,96,576]{3,2,1,0:T(8,128)(2,1)S(1)} collective-permute-done((bf16[2,2,96,576]{3,2,1,0:T(8,128)(2,1)S(1)}, bf16[2,2,96,576]{3,2,1,0:T(8,128)(2,1)S(1)}, u32[]{:S(2)}, u32[]{:S(2)}) %collective-permute-start.33) | collective-permute-done | bytes 442400 | tf_op jit(solution)/shard_map/ppermute | solution.py:562
  236.2 5.0 %collective-permute-done.34 = bf16[2,96,576]{2,1,0:T(8,128)(2,1)S(1)} collective-permute-done((bf16[2,96,576]{2,1,0:T(8,128)(2,1)S(1)}, bf16[2,96,576]{2,1,0:T(8,128)(2,1)S(1)}, u32[]{:S(2)}, u32[]{:S(2)}) %collective-permute-start.34) | collective-permute-done | bytes 221216 | tf_op jit(solution)/shard_map/ppermute | solution.py:562
  241.3 1.8 collective-permute-done.44
  243.1 3.7 %collective-permute-start.35 = (bf16[96,576]{1,0:T(8,128)(2,1)S(1)}, bf16[96,576]{1,0:T(8,128)(2,1)S(1)}, u32[]{:S(2)}, u32[]{:S(2)}) collective-permute-start(bf16[96,576]{1,0:T(8,128)(2,1)S(1)} %fusion.8), channel_id=1, source_target_pairs={{0,16},{4,20},{8,24},{12,28},{16,0},{20,4},{24,8},{28,12},{1,17},{... | collective-permute-start | bytes 331784 | tf_op jit(solution)/shard_map/ppermute | solution.py:562
  247.6 3.0 %collective-permute-done.35 = bf16[96,576]{1,0:T(8,128)(2,1)S(1)} collective-permute-done((bf16[96,576]{1,0:T(8,128)(2,1)S(1)}, bf16[96,576]{1,0:T(8,128)(2,1)S(1)}, u32[]{:S(2)}, u32[]{:S(2)}) %collective-permute-start.35) | collective-permute-done | bytes 110624 | tf_op jit(solution)/shard_map/ppermute | solution.py:562
  250.6 2.2 collective-permute-start.45
  256.9 1.6 collective-permute-start.50
  263.9 3.4 %collective-permute-done.50 = bf16[192,384]{1,0:T(8,128)(2,1)} collective-permute-done((bf16[192,384]{1,0:T(8,128)(2,1)S(1)}, bf16[192,384]{1,0:T(8,128)(2,1)}, u32[]{:S(2)}, u32[]{:S(2)}) %collective-permute-start.50) | collective-permute-done | bytes 147488 | tf_op jit(solution)/shard_map/ppermute | solution.py:562
  269.9 10.2 %collective-permute-done.46 = bf16[48,1920]{1,0:T(8,128)(2,1)S(1)} collective-permute-done((bf16[48,1920]{1,0:T(8,128)(2,1)S(1)}, bf16[48,1920]{1,0:T(8,128)(2,1)S(1)}, u32[]{:S(2)}, u32[]{:S(2)}) %collective-permute-start.46) | collective-permute-done | bytes 184352 | tf_op jit(solution)/shard_map/ppermute | solution.py:562
  282.1 5.4 %collective-permute-done.22.refs_2_ = bf16[1,256,768]{2,1,0:T(8,128)(2,1)S(1)} collective-permute-done((bf16[1,256,768]{2,1,0:T(8,128)(2,1)}, bf16[1,256,768]{2,1,0:T(8,128)(2,1)S(1)}, u32[]{:S(2)}, u32[]{:S(2)}) %collective-permute-start.22) | collective-permute-done | bytes 393248 | tf_op jit(solution)/shard_map/ppermute | solution.py:635
  288.3 5.8 %finish_tokens.1 = bf16[3,256,768]{2,1,0:T(8,128)(2,1)} custom-call(bf16[3,256,768]{2,1,0:T(8,128)(2,1)} %x.1, f32[768,768]{1,0:T(8,128)} %get-tuple-element.84.gmid, f32[1,768]{1,0:T(1,128)} %slice.240.gain, bf16[2,256,768]{2,1,0:T(8,128)(2,1)} %get-tuple-element.93.refs_0_, bf16[2,256,768]{2,1,0:T(8,128)(2,1)} %copy-done.5, ...), custom_call_target="tpu_custom_call" | custom-call | tf_op jit(solution)/shard_map/finish_tokens/pallas_call | solution.py:534
  (299 shorter events, 61.4 us)
Async XLA Ops:
  2.1 13.1 %collective-permute-start.13 = (bf16[256,768]{1,0:T(8,128)(2,1)S(1)}, bf16[256,768]{1,0:T(8,128)(2,1)}, u32[]{:S(2)}, u32[]{:S(2)}) collective-permute-start(bf16[256,768]{1,0:T(8,128)(2,1)S(1)} %get-tuple-element.134.refs_0_), channel_id=1, source_target_pairs={{0,2},{1,3},{2,0},{3,1},{4,6},{5,7},{6,4},{7,5},{8,10},{9,11},{10,... | collective-permute-start | bytes 1179656 | tf_op jit(solution)/shard_map/ppermute | solution.py:635
  5.1 21.7 %collective-permute-start.12 = (bf16[256,768]{1,0:T(8,128)(2,1)S(1)}, bf16[256,768]{1,0:T(8,128)(2,1)}, u32[]{:S(2)}, u32[]{:S(2)}) collective-permute-start(bf16[256,768]{1,0:T(8,128)(2,1)S(1)} %get-tuple-element.134.refs_0_), channel_id=1, source_target_pairs={{0,1},{1,0},{2,3},{3,2},{4,5},{5,4},{6,7},{7,6},{8,9},{9,8},{10,11... | collective-permute-start | bytes 1179656 | tf_op jit(solution)/shard_map/ppermute | solution.py:635
  5.1 18.4 %collective-permute-start.7 = (bf16[256,768]{1,0:T(8,128)(2,1)S(1)}, bf16[256,768]{1,0:T(8,128)(2,1)S(1)}, u32[]{:S(2)}, u32[]{:S(2)}) collective-permute-start(bf16[256,768]{1,0:T(8,128)(2,1)S(1)} %get-tuple-element.135.refs_0_), channel_id=1, source_target_pairs={{0,2},{1,3},{2,0},{3,1},{4,6},{5,7},{6,4},{7,5},{8,10},{9,11},{10,... | collective-permute-start | bytes 1179656 | tf_op jit(solution)/shard_map/ppermute | solution.py:635
  5.3 48.9 %collective-permute-start.6 = (bf16[256,768]{1,0:T(8,128)(2,1)S(1)}, bf16[256,768]{1,0:T(8,128)(2,1)}, u32[]{:S(2)}, u32[]{:S(2)}) collective-permute-start(bf16[256,768]{1,0:T(8,128)(2,1)S(1)} %get-tuple-element.135.refs_0_), channel_id=1, source_target_pairs={{0,1},{1,0},{2,3},{3,2},{4,5},{5,4},{6,7},{7,6},{8,9},{9,8},{10,11... | collective-permute-start | bytes 1179656 | tf_op jit(solution)/shard_map/ppermute | solution.py:635
  5.6 25.5 %collective-permute-start.1 = (bf16[256,768]{1,0:T(8,128)(2,1)S(1)}, bf16[256,768]{1,0:T(8,128)(2,1)S(1)}, u32[]{:S(2)}, u32[]{:S(2)}) collective-permute-start(bf16[256,768]{1,0:T(8,128)(2,1)S(1)} %get-tuple-element.136.refs_0_), channel_id=1, source_target_pairs={{0,2},{1,3},{2,0},{3,1},{4,6},{5,7},{6,4},{7,5},{8,10},{9,11},{10,... | collective-permute-start | bytes 1179656 | tf_op jit(solution)/shard_map/ppermute | solution.py:635
  15.2 15.9 %collective-permute-start.14 = (bf16[256,768]{1,0:T(8,128)(2,1)}, bf16[256,768]{1,0:T(8,128)(2,1)}, u32[]{:S(2)}, u32[]{:S(2)}) collective-permute-start(bf16[256,768]{1,0:T(8,128)(2,1)} %collective-permute-done.13.refs_2_), channel_id=1, source_target_pairs={{0,1},{1,0},{2,3},{3,2},{4,5},{5,4},{6,7},{7,6},{8,9},{9,8},{10,11... | collective-permute-start | bytes 1179656 | tf_op jit(solution)/shard_map/ppermute | solution.py:635
  23.5 32.4 %collective-permute-start.8 = (bf16[256,768]{1,0:T(8,128)(2,1)S(1)}, bf16[256,768]{1,0:T(8,128)(2,1)}, u32[]{:S(2)}, u32[]{:S(2)}) collective-permute-start(bf16[256,768]{1,0:T(8,128)(2,1)S(1)} %collective-permute-done.7.refs_2_), channel_id=1, source_target_pairs={{0,1},{1,0},{2,3},{3,2},{4,5},{5,4},{6,7},{7,6},{8,9},{9,8},{10,11... | collective-permute-start | bytes 1179656 | tf_op jit(solution)/shard_map/ppermute | solution.py:635
  26.9 42.4 %collective-permute-start = (bf16[256,768]{1,0:T(8,128)(2,1)S(1)}, bf16[256,768]{1,0:T(8,128)(2,1)S(1)}, u32[]{:S(2)}, u32[]{:S(2)}) collective-permute-start(bf16[256,768]{1,0:T(8,128)(2,1)S(1)} %get-tuple-element.136.refs_0_), channel_id=1, source_target_pairs={{0,1},{1,0},{2,3},{3,2},{4,5},{5,4},{6,7},{7,6},{8,9},{9,8},{10,11... | collective-permute-start | bytes 1179656 | tf_op jit(solution)/shard_map/ppermute | solution.py:635
  31.1 39.7 %collective-permute-start.2 = (bf16[256,768]{1,0:T(8,128)(2,1)S(1)}, bf16[256,768]{1,0:T(8,128)(2,1)S(1)}, u32[]{:S(2)}, u32[]{:S(2)}) collective-permute-start(bf16[256,768]{1,0:T(8,128)(2,1)S(1)} %collective-permute-done.1.refs_2_), channel_id=1, source_target_pairs={{0,1},{1,0},{2,3},{3,2},{4,5},{5,4},{6,7},{7,6},{8,9},{9,8},{10,11... | collective-permute-start | bytes 1179656 | tf_op jit(solution)/shard_map/ppermute | solution.py:635
  53.7 25.5 %collective-permute-start.15 = (bf16[192,256]{1,0:T(8,128)(2,1)}, bf16[192,256]{1,0:T(8,128)(2,1)S(1)}, u32[]{:S(2)}, u32[]{:S(2)}) collective-permute-start(bf16[192,256]{1,0:T(8,128)(2,1)} %get-tuple-element.80), channel_id=1, source_target_pairs={{0,1},{1,0},{2,3},{3,2},{4,5},{5,4},{6,7},{7,6},{8,9},{9,8},{10,11... | collective-permute-start | bytes 294920 | tf_op jit(solution)/shard_map/ppermute | solution.py:635
  54.2 25.5 %collective-permute-start.16 = (bf16[192,256]{1,0:T(8,128)(2,1)}, bf16[192,256]{1,0:T(8,128)(2,1)S(1)}, u32[]{:S(2)}, u32[]{:S(2)}) collective-permute-start(bf16[192,256]{1,0:T(8,128)(2,1)} %get-tuple-element.81), channel_id=1, source_target_pairs={{0,2},{1,3},{2,0},{3,1},{4,6},{5,7},{6,4},{7,5},{8,10},{9,11},{10,... | collective-permute-start | bytes 294920 | tf_op jit(solution)/shard_map/ppermute | solution.py:635
  55.9 23.9 %collective-permute-start.17 = (bf16[192,256]{1,0:T(8,128)(2,1)}, bf16[192,256]{1,0:T(8,128)(2,1)S(1)}, u32[]{:S(2)}, u32[]{:S(2)}) collective-permute-start(bf16[192,256]{1,0:T(8,128)(2,1)} %get-tuple-element.82), channel_id=1, source_target_pairs={{0,3},{1,2},{2,1},{3,0},{4,7},{5,6},{6,5},{7,4},{8,11},{9,10},{10,... | collective-permute-start | bytes 294920 | tf_op jit(solution)/shard_map/ppermute | solution.py:635
  69.3 11.9 %collective-permute-start.10 = (bf16[192,256]{1,0:T(8,128)(2,1)}, bf16[192,256]{1,0:T(8,128)(2,1)S(1)}, u32[]{:S(2)}, u32[]{:S(2)}) collective-permute-start(bf16[192,256]{1,0:T(8,128)(2,1)} %get-tuple-element.77), channel_id=1, source_target_pairs={{0,2},{1,3},{2,0},{3,1},{4,6},{5,7},{6,4},{7,5},{8,10},{9,11},{10,... | collective-permute-start | bytes 294920 | tf_op jit(solution)/shard_map/ppermute | solution.py:635
  70.8 11.3 %collective-permute-start.11 = (bf16[192,256]{1,0:T(8,128)(2,1)}, bf16[192,256]{1,0:T(8,128)(2,1)S(1)}, u32[]{:S(2)}, u32[]{:S(2)}) collective-permute-start(bf16[192,256]{1,0:T(8,128)(2,1)} %get-tuple-element.78), channel_id=1, source_target_pairs={{0,3},{1,2},{2,1},{3,0},{4,7},{5,6},{6,5},{7,4},{8,11},{9,10},{10,... | collective-permute-start | bytes 294920 | tf_op jit(solution)/shard_map/ppermute | solution.py:635
  151.1 20.9 %collective-permute-start.23 = (bf16[192,256]{1,0:T(8,128)(2,1)}, bf16[192,256]{1,0:T(8,128)(2,1)S(1)}, u32[]{:S(2)}, u32[]{:S(2)}) collective-permute-start(bf16[192,256]{1,0:T(8,128)(2,1)} %get-tuple-element.96), channel_id=1, source_target_pairs={{0,1},{1,0},{2,3},{3,2},{4,5},{5,4},{6,7},{7,6},{8,9},{9,8},{10,11... | collective-permute-start | bytes 294920 | tf_op jit(solution)/shard_map/ppermute | solution.py:635
  151.4 20.7 %collective-permute-start.24 = (bf16[192,256]{1,0:T(8,128)(2,1)}, bf16[192,256]{1,0:T(8,128)(2,1)S(1)}, u32[]{:S(2)}, u32[]{:S(2)}) collective-permute-start(bf16[192,256]{1,0:T(8,128)(2,1)} %get-tuple-element.97), channel_id=1, source_target_pairs={{0,2},{1,3},{2,0},{3,1},{4,6},{5,7},{6,4},{7,5},{8,10},{9,11},{10,... | collective-permute-start | bytes 294920 | tf_op jit(solution)/shard_map/ppermute | solution.py:635
  156.9 15.2 %collective-permute-start.25 = (bf16[192,256]{1,0:T(8,128)(2,1)}, bf16[192,256]{1,0:T(8,128)(2,1)S(1)}, u32[]{:S(2)}, u32[]{:S(2)}) collective-permute-start(bf16[192,256]{1,0:T(8,128)(2,1)} %get-tuple-element.98), channel_id=1, source_target_pairs={{0,3},{1,2},{2,1},{3,0},{4,7},{5,6},{6,5},{7,4},{8,11},{9,10},{10,... | collective-permute-start | bytes 294920 | tf_op jit(solution)/shard_map/ppermute | solution.py:635
  157.1 33.1 %collective-permute-start.28 = (bf16[192,256]{1,0:T(8,128)(2,1)}, bf16[192,256]{1,0:T(8,128)(2,1)S(1)}, u32[]{:S(2)}, u32[]{:S(2)}) collective-permute-start(bf16[192,256]{1,0:T(8,128)(2,1)} %get-tuple-element.108), channel_id=1, source_target_pairs={{0,1},{1,0},{2,3},{3,2},{4,5},{5,4},{6,7},{7,6},{8,9},{9,8},{10,11... | collective-permute-start | bytes 294920 | tf_op jit(solution)/shard_map/ppermute | solution.py:635
  157.8 32.5 %collective-permute-start.29 = (bf16[192,256]{1,0:T(8,128)(2,1)}, bf16[192,256]{1,0:T(8,128)(2,1)S(1)}, u32[]{:S(2)}, u32[]{:S(2)}) collective-permute-start(bf16[192,256]{1,0:T(8,128)(2,1)} %get-tuple-element.109), channel_id=1, source_target_pairs={{0,2},{1,3},{2,0},{3,1},{4,6},{5,7},{6,4},{7,5},{8,10},{9,11},{10,... | collective-permute-start | bytes 294920 | tf_op jit(solution)/shard_map/ppermute | solution.py:635
  172.0 18.3 %collective-permute-start.30 = (bf16[192,256]{1,0:T(8,128)(2,1)S(1)}, bf16[192,256]{1,0:T(8,128)(2,1)S(1)}, u32[]{:S(2)}, u32[]{:S(2)}) collective-permute-start(bf16[192,256]{1,0:T(8,128)(2,1)S(1)} %copy-done.37), channel_id=1, source_target_pairs={{0,3},{1,2},{2,1},{3,0},{4,7},{5,6},{6,5},{7,4},{8,11},{9,10},{10,... | collective-permute-start | bytes 294920 | tf_op jit(solution)/shard_map/ppermute | solution.py:635
  212.8 22.1 %collective-permute-start.48 = (bf16[2,2,192,384]{3,2,0,1:T(8,128)(2,1)S(1)}, bf16[2,2,192,384]{3,2,0,1:T(8,128)(2,1)S(1)}, u32[]{:S(2)}, u32[]{:S(2)}) collective-permute-start(bf16[2,2,192,384]{3,2,0,1:T(8,128)(2,1)S(1)} %copy_bitcast_fusion.1), channel_id=1, source_target_pairs={{0,2},{1,3},{2,0},{3,1},{4,6},{5,7},{6,4},{7,5},{8,10},{9,11},{10,... | collective-permute-start | bytes 1769480 | tf_op jit(solution)/shard_map/ppermute | solution.py:562
  218.7 24.4 %collective-permute-start.44 = (bf16[2,2,48,1920]{3,2,0,1:T(8,128)(2,1)S(1)}, bf16[2,2,48,1920]{3,2,0,1:T(8,128)(2,1)S(1)}, u32[]{:S(2)}, u32[]{:S(2)}) collective-permute-start(bf16[2,2,48,1920]{3,2,0,1:T(8,128)(2,1)S(1)} %copy_bitcast_fusion), channel_id=1, source_target_pairs={{0,2},{1,3},{2,0},{3,1},{4,6},{5,7},{6,4},{7,5},{8,10},{9,11},{10,... | collective-permute-start | bytes 2211848 | tf_op jit(solution)/shard_map/ppermute | solution.py:562
  223.9 30.2 %collective-permute-start.31 = (bf16[2,256,768]{2,1,0:T(8,128)(2,1)S(1)}, bf16[2,256,768]{2,1,0:T(8,128)(2,1)S(1)}, u32[]{:S(2)}, u32[]{:S(2)}) collective-permute-start(bf16[2,256,768]{2,1,0:T(8,128)(2,1)S(1)} %copy-done.32), channel_id=1, source_target_pairs={{0,1},{1,0},{2,3},{3,2},{4,5},{5,4},{6,7},{7,6},{8,9},{9,8},{10,11... | collective-permute-start | bytes 2359304 | tf_op jit(solution)/shard_map/ppermute | solution.py:635
  225.3 30.4 %collective-permute-start.26 = (bf16[2,256,768]{2,1,0:T(8,128)(2,1)S(1)}, bf16[2,256,768]{2,1,0:T(8,128)(2,1)S(1)}, u32[]{:S(2)}, u32[]{:S(2)}) collective-permute-start(bf16[2,256,768]{2,1,0:T(8,128)(2,1)S(1)} %copy-done.31), channel_id=1, source_target_pairs={{0,1},{1,0},{2,3},{3,2},{4,5},{5,4},{6,7},{7,6},{8,9},{9,8},{10,11... | collective-permute-start | bytes 2359304 | tf_op jit(solution)/shard_map/ppermute | solution.py:635
  234.9 22.0 %collective-permute-start.21 = (bf16[2,256,768]{2,1,0:T(8,128)(2,1)S(1)}, bf16[2,256,768]{2,1,0:T(8,128)(2,1)S(1)}, u32[]{:S(2)}, u32[]{:S(2)}) collective-permute-start(bf16[2,256,768]{2,1,0:T(8,128)(2,1)S(1)} %copy-done.30), channel_id=1, source_target_pairs={{0,1},{1,0},{2,3},{3,2},{4,5},{5,4},{6,7},{7,6},{8,9},{9,8},{10,11... | collective-permute-start | bytes 2359304 | tf_op jit(solution)/shard_map/ppermute | solution.py:635
  241.2 11.6 %collective-permute-start.49 = (bf16[2,192,384]{2,1,0:T(8,128)(2,1)S(1)}, bf16[2,192,384]{2,1,0:T(8,128)(2,1)S(1)}, u32[]{:S(2)}, u32[]{:S(2)}) collective-permute-start(bf16[2,192,384]{2,1,0:T(8,128)(2,1)S(1)} %fusion.1), channel_id=1, source_target_pairs={{0,8},{4,12},{8,0},{12,4},{16,24},{20,28},{24,16},{28,20},{1,9},{5... | collective-permute-start | bytes 884744 | tf_op jit(solution)/shard_map/ppermute | solution.py:562
  250.6 18.1 %collective-permute-start.45 = (bf16[2,48,1920]{2,1,0:T(8,128)(2,1)}, bf16[2,48,1920]{2,1,0:T(8,128)(2,1)}, u32[]{:S(2)}, u32[]{:S(2)}) collective-permute-start(bf16[2,48,1920]{2,1,0:T(8,128)(2,1)} %fusion), channel_id=1, source_target_pairs={{0,4},{4,0},{8,12},{12,8},{16,20},{20,16},{24,28},{28,24},{1,5},{5... | collective-permute-start | bytes 1105928 | tf_op jit(solution)/shard_map/ppermute | solution.py:562
  256.9 10.3 %collective-permute-start.50 = (bf16[192,384]{1,0:T(8,128)(2,1)S(1)}, bf16[192,384]{1,0:T(8,128)(2,1)}, u32[]{:S(2)}, u32[]{:S(2)}) collective-permute-start(bf16[192,384]{1,0:T(8,128)(2,1)S(1)} %fusion.6), channel_id=1, source_target_pairs={{0,16},{4,20},{8,24},{12,28},{16,0},{20,4},{24,8},{28,12},{1,17},{... | collective-permute-start | bytes 442376 | tf_op jit(solution)/shard_map/ppermute | solution.py:562
  259.4 22.7 %collective-permute-start.32 = (bf16[1,256,768]{2,1,0:T(8,128)(2,1)S(1)}, bf16[1,256,768]{2,1,0:T(8,128)(2,1)S(1)}, u32[]{:S(2)}, u32[]{:S(2)}) collective-permute-start(bf16[1,256,768]{2,1,0:T(8,128)(2,1)S(1)} %add_convert_fusion), channel_id=1, source_target_pairs={{0,2},{1,3},{2,0},{3,1},{4,6},{5,7},{6,4},{7,5},{8,10},{9,11},{10,... | collective-permute-start | bytes 1179656 | tf_op jit(solution)/shard_map/ppermute | solution.py:635
  260.8 21.3 %collective-permute-start.27 = (bf16[1,256,768]{2,1,0:T(8,128)(2,1)}, bf16[1,256,768]{2,1,0:T(8,128)(2,1)S(1)}, u32[]{:S(2)}, u32[]{:S(2)}) collective-permute-start(bf16[1,256,768]{2,1,0:T(8,128)(2,1)} %add_convert_fusion.1), channel_id=1, source_target_pairs={{0,2},{1,3},{2,0},{3,1},{4,6},{5,7},{6,4},{7,5},{8,10},{9,11},{10,... | collective-permute-start | bytes 1179656 | tf_op jit(solution)/shard_map/ppermute | solution.py:635
  261.5 26.0 %collective-permute-start.22 = (bf16[1,256,768]{2,1,0:T(8,128)(2,1)}, bf16[1,256,768]{2,1,0:T(8,128)(2,1)S(1)}, u32[]{:S(2)}, u32[]{:S(2)}) collective-permute-start(bf16[1,256,768]{2,1,0:T(8,128)(2,1)} %add_convert_fusion.2), channel_id=1, source_target_pairs={{0,2},{1,3},{2,0},{3,1},{4,6},{5,7},{6,4},{7,5},{8,10},{9,11},{10,... | collective-permute-start | bytes 1179656 | tf_op jit(solution)/shard_map/ppermute | solution.py:635
  281.2 12.9 %collective-permute-start.47 = (bf16[24,1920]{1,0:T(8,128)(2,1)S(1)}, bf16[24,1920]{1,0:T(8,128)(2,1)S(1)}, u32[]{:S(2)}, u32[]{:S(2)}) collective-permute-start(bf16[24,1920]{1,0:T(8,128)(2,1)S(1)} %fusion.10), channel_id=1, source_target_pairs={{0,1},{1,0},{2,3},{3,2},{4,5},{5,4},{6,7},{7,6},{8,9},{9,8},{10,11... | collective-permute-start | bytes 276488 | tf_op jit(solution)/shard_map/ppermute | solution.py:635
  (77 other events, 712.9 us)
